TPU v7x, 32 devices: a whole 2x2x4 slice. The times are simulated.
32 devices in a mesh: seq: 8 (over y, x, core), heads: 4 (over z).
Axes of the slice: x: 2, y: 2, z: 4, core: 2. Of those that a mesh axis runs over, the one named last changes fastest.
Arguments:
- tokens: bfloat16 [2, 2048, 2048], P(None, 'seq'), may hold values from -6 to 6
- attn_gain: float32 [2048], replicated, may hold values from 0.5 to 1.5
- base_qkv: bfloat16 [3, 2048, 2048], P(None, None, 'heads'), may hold values from -0.125 to 0.125
- adapt_a_qkv: bfloat16 [3, 2048, 16], replicated, may hold values from -0.125 to 0.125
- adapt_b_qkv: bfloat16 [3, 16, 2048], P(None, None, 'heads'), may hold values from -0.375 to 0.375
- magnitude_qkv: float32 [3, 2048], P(None, 'heads'), may hold values from 0.7 to 1.8
- base_out: bfloat16 [2048, 2048], P('heads'), may hold values from -0.125 to 0.125
- adapt_a_out: bfloat16 [2048, 16], P('heads'), may hold values from -0.125 to 0.125
- adapt_b_out: bfloat16 [16, 2048], replicated, may hold values from -0.375 to 0.375
- magnitude_out: float32 [2048], replicated, may hold values from 4 to 16
- ffn_gain: float32 [2048], replicated, may hold values from 0.5 to 1.5
- base_gu: bfloat16 [2, 2048, 5632], P(None, None, 'heads'), may hold values from -0.125 to 0.125
- adapt_a_gu: bfloat16 [2, 2048, 16], replicated, may hold values from -0.125 to 0.125
- adapt_b_gu: bfloat16 [2, 16, 5632], P(None, None, 'heads'), may hold values from -0.375 to 0.375
- magnitude_gu: float32 [2, 5632], P(None, 'heads'), may hold values from 0.5 to 2
- base_down: bfloat16 [5632, 2048], P('heads'), may hold values from -0.078125 to 0.078125
- adapt_a_down: bfloat16 [5632, 16], P('heads'), may hold values from -0.078125 to 0.078125
- adapt_b_down: bfloat16 [16, 2048], replicated, may hold values from -0.375 to 0.375
- magnitude_down: float32 [2048], replicated, may hold values from 1 to 4
- doc_lengths: int32 [2, 8], replicated, may hold values from 1 to 1536, 2048 in all within a row
- cotangent: bfloat16 [2, 2048, 2048], P(None, 'seq'), may hold values from -6 to 6
Outputs:
- mixed: bfloat16 [2, 2048, 2048], P(None, 'seq')
- grad_tokens: float32 [2, 2048, 2048], P(None, 'seq')
- grad_attn_gain: float32 [2048], replicated
- grad_a_qkv: float32 [3, 2048, 16], replicated
- grad_b_qkv: float32 [3, 16, 2048], P(None, None, 'heads')
- grad_m_qkv: float32 [3, 2048], P(None, 'heads')
- grad_a_out: float32 [2048, 16], P('heads')
- grad_b_out: float32 [16, 2048], replicated
- grad_m_out: float32 [2048], replicated
- grad_ffn_gain: float32 [2048], replicated
- grad_a_gu: float32 [2, 2048, 16], replicated
- grad_b_gu: float32 [2, 16, 5632], P(None, None, 'heads')
- grad_m_gu: float32 [2, 5632], P(None, 'heads')
- grad_a_down: float32 [5632, 16], P('heads')
- grad_b_down: float32 [16, 2048], replicated
- grad_m_down: float32 [2048], replicated
Inputs may be any that keep to these rules, and one draw needn't show every extreme that they name: `doc_lengths`: each row's 8 lengths sum to 2048, and the longest of each row is exactly 1536.
All inputs are finite; a program needn't handle non-finite values.
Results may differ from a plain program's by a relative error of at most 0.029.
Values may be sent and summed in bfloat16 or wider, within the bound.
A program may use at most 448 MiB of HBM per device.

v0:
```python
import jax
import jax.numpy as jnp
from jax import lax
from jax.sharding import PartitionSpec as P

HD = 128


ADAPT_SCALE = 2.0
NORM_EPS = 1e-05
COLUMN_EPS = 1e-06
ROPE_BASE = 10000.0
NEG_LARGE = -1e30
FULL_PRECISION = lax.Precision.HIGHEST
WIDE_TYPE = jnp.float32
NARROW_TYPE = jnp.bfloat16


def doc_layout(doc_lengths, start_at, span_rows):
    doc_ends = jnp.cumsum(doc_lengths, axis=1)
    starts = doc_ends - doc_lengths
    places = start_at + jnp.arange(span_rows, dtype=jnp.int32)
    passed = places[None, :, None] >= doc_ends[:, None, :]
    segment = jnp.sum(passed.astype(jnp.int32), axis=2)
    inside = jnp.logical_and(places[None, :, None] >= starts[:, None, :], jnp.logical_not(passed))
    offsets = jnp.sum(jnp.where(inside, starts[:, None, :], 0), axis=2)
    row_places = jnp.broadcast_to(places[None, :], segment.shape)
    return (segment, row_places - offsets, row_places)


def touches(doc_lengths, query_low, query_high, key_low, key_high):
    doc_ends = jnp.cumsum(doc_lengths, axis=1)
    seg_key = jnp.sum((key_high >= doc_ends).astype(jnp.int32), axis=1)
    seg_query = jnp.sum((query_low >= doc_ends).astype(jnp.int32), axis=1)
    reach = jnp.logical_or(key_high >= query_low, seg_key == seg_query)
    return jnp.any(jnp.logical_and(key_low <= query_high, reach))


def visible_mask(seg_query, place_query, seg_key, place_key):
    same_doc = seg_query[:, :, None] == seg_key[:, None, :]
    causal = place_key[:, None, :] <= place_query[:, :, None]
    return jnp.logical_and(same_doc, causal)[:, None]


def rope_tables(positions, head_size):
    half_size = head_size // 2
    frequency = ROPE_BASE ** (jnp.arange(half_size, dtype=WIDE_TYPE) * (-2.0 / head_size))
    angles = positions.astype(WIDE_TYPE)[..., None] * frequency
    return (jnp.cos(angles)[:, :, None, :], jnp.sin(angles)[:, :, None, :])


def rotate(values, cosine, sine_t):
    half_size = values.shape[-1] // 2
    first_half = values[..., :half_size]
    second_half = values[..., half_size:]
    return jnp.concatenate(
        [first_half * cosine - second_half * sine_t, second_half * cosine + first_half * sine_t],
        axis=-1,
    )


def rotate_back(grads_in, cosine, sine_t):
    half_size = grads_in.shape[-1] // 2
    first_half = grads_in[..., :half_size]
    second_half = grads_in[..., half_size:]
    return jnp.concatenate(
        [first_half * cosine + second_half * sine_t, second_half * cosine - first_half * sine_t],
        axis=-1,
    )


def rms_back(values, inverse, gain_vec, grad_in):
    scaled = grad_in * gain_vec
    grad_values = inverse * scaled - values * inverse**3 * jnp.mean(
        scaled * values, axis=-1, keepdims=True
    )
    return (grad_values, jnp.sum(grad_in * values * inverse, axis=0))


def block_scores(query_b, key_b):
    return jnp.einsum(
        "rqhd,rkhd->rhqk", query_b, key_b, preferred_element_type=WIDE_TYPE
    ) * query_b.shape[3] ** (-0.5)


def block_grads(query_b, key_blk, value_blk, grad_out_b, log_sum, delta_row, visible):
    scores = block_scores(query_b, key_blk)
    probs = jnp.exp(jnp.where(visible, scores - log_sum[..., None], NEG_LARGE))
    grad_probs = jnp.einsum(
        "rqhd,rkhd->rhqk", grad_out_b, value_blk, preferred_element_type=WIDE_TYPE
    )
    grad_scores = (probs * (grad_probs - delta_row[..., None])).astype(NARROW_TYPE)
    return (probs.astype(NARROW_TYPE), grad_scores)


def project_columns(inputs_b, base_w, adapt_a, adapt_b):
    full_weight = base_w.astype(WIDE_TYPE) + ADAPT_SCALE * jnp.dot(
        adapt_a.astype(WIDE_TYPE), adapt_b.astype(WIDE_TYPE), precision=FULL_PRECISION
    )
    col_norm = jnp.sqrt(jnp.sum(full_weight * full_weight, axis=0) + COLUMN_EPS)
    low_rank = jnp.dot(inputs_b, adapt_a, preferred_element_type=WIDE_TYPE).astype(NARROW_TYPE)
    pre_act = jnp.dot(inputs_b, base_w, preferred_element_type=WIDE_TYPE) + ADAPT_SCALE * jnp.dot(
        low_rank, adapt_b, preferred_element_type=WIDE_TYPE
    )
    return (pre_act, low_rank, col_norm, full_weight)


def column_back(grad_out, pre_act, col_scale, low_rank, base_w, adapt_b):
    col_sums = jnp.sum(grad_out * pre_act, axis=0)
    grad_pre = (grad_out * col_scale).astype(NARROW_TYPE)
    d_low = ADAPT_SCALE * jnp.einsum(
        "tc,rc->tr", grad_pre, adapt_b, preferred_element_type=WIDE_TYPE
    )
    d_input = jnp.einsum("tc,ic->ti", grad_pre, base_w, preferred_element_type=WIDE_TYPE)
    grad_b = ADAPT_SCALE * jnp.einsum(
        "tr,tc->rc", low_rank, grad_pre, preferred_element_type=WIDE_TYPE
    )
    return (col_sums, d_input, d_low, grad_b, grad_pre)


def norm_path(full_weight, adapt_a_f, adapt_b_f, magnitude, col_norm, col_total):
    weight_grad = (
        full_weight * (-(magnitude * col_total) / (col_norm * col_norm * col_norm))[None, :]
    )
    grad_a = ADAPT_SCALE * jnp.dot(weight_grad, adapt_b_f.T, precision=FULL_PRECISION)
    grad_b = ADAPT_SCALE * jnp.dot(adapt_a_f.T, weight_grad, precision=FULL_PRECISION)
    return (grad_a, grad_b, col_total / col_norm)


def unchanged(state_now):
    return state_now


def per_device(
    tokens,
    attn_gain,
    base_qkv,
    adapt_a_qkv,
    adapt_b_qkv,
    magnitude_qkv,
    base_out,
    adapt_a_out,
    adapt_b_out,
    magnitude_out,
    ffn_gain,
    base_gu,
    adapt_a_gu,
    adapt_b_gu,
    magnitude_gu,
    base_down,
    adapt_a_down,
    adapt_b_down,
    magnitude_down,
    doc_lengths,
    cotangent,
):
    rows_n, group_len, model_width = tokens.shape
    token_count = rows_n * group_len
    local_width = base_qkv.shape[2]
    heads_here = local_width // HD
    row_len = group_len * lax.axis_size("seq")
    group_start = lax.axis_index("seq") * group_len
    key_block = min(512, row_len)
    block_count = row_len // key_block
    key_scale = HD ** (-0.5)
    segment_q, position_q, place_q = doc_layout(doc_lengths, group_start, group_len)
    cosine, sine_t = rope_tables(position_q, HD)
    inputs = tokens.astype(WIDE_TYPE).reshape(token_count, model_width)
    inverse_one = lax.rsqrt(jnp.mean(inputs * inputs, axis=-1, keepdims=True) + NORM_EPS)
    normed_b = (inputs * inverse_one * attn_gain).astype(NARROW_TYPE)
    qkv_parts = [
        project_columns(normed_b, base_qkv[slot_at], adapt_a_qkv[slot_at], adapt_b_qkv[slot_at])
        for slot_at in range(3)
    ]
    qkv_scale = [magnitude_qkv[slot_at] / qkv_parts[slot_at][2] for slot_at in range(3)]
    shaped = [
        (qkv_parts[slot_at][0] * qkv_scale[slot_at]).reshape(rows_n, group_len, heads_here, HD)
        for slot_at in range(3)
    ]
    query_b = rotate(shaped[0], cosine, sine_t).astype(NARROW_TYPE)
    key_b = (
        rotate(shaped[1], cosine, sine_t)
        .astype(NARROW_TYPE)
        .reshape(rows_n, group_len, local_width)
    )
    value_b = shaped[2].astype(NARROW_TYPE).reshape(rows_n, group_len, local_width)
    keys_all, values_all = (
        lax.all_gather(key_b, "seq", axis=1, tiled=True),
        lax.all_gather(value_b, "seq", axis=1, tiled=True),
    )

    def key_slice(block_index):
        key_start = block_index * key_block
        key_blk = lax.dynamic_slice_in_dim(keys_all, key_start, key_block, 1).reshape(
            rows_n, key_block, heads_here, HD
        )
        value_blk = lax.dynamic_slice_in_dim(values_all, key_start, key_block, 1).reshape(
            rows_n, key_block, heads_here, HD
        )
        seg_key, unused, place_key = doc_layout(doc_lengths, key_start, key_block)
        visible = visible_mask(segment_q, place_q, seg_key, place_key)
        nearby = touches(
            doc_lengths,
            group_start,
            group_start + group_len - 1,
            key_start,
            key_start + key_block - 1,
        )
        return (key_blk, value_blk, visible, nearby)

    def stats_step(running, block_index):
        key_blk, value_blk, visible, nearby = key_slice(block_index)

        def stats_accumulate(state_now):
            row_top, total_sum = state_now
            masked = jnp.where(visible, block_scores(query_b, key_blk), NEG_LARGE)
            new_top = jnp.maximum(row_top, jnp.max(masked, axis=3))
            shifted = jnp.where(visible, masked - new_top[..., None], NEG_LARGE)
            return (
                new_top,
                total_sum * jnp.exp(row_top - new_top) + jnp.sum(jnp.exp(shifted), axis=3),
            )

        return (lax.cond(nearby, stats_accumulate, unchanged, running), None)

    start_stats = (
        jnp.full((rows_n, heads_here, group_len), NEG_LARGE, WIDE_TYPE),
        jnp.zeros((rows_n, heads_here, group_len), WIDE_TYPE),
    )
    (row_top, total_sum), unused = lax.scan(
        stats_step, start_stats, jnp.arange(block_count, dtype=jnp.int32)
    )
    log_sum = row_top + jnp.log(total_sum)

    def output_step(running, block_index):
        key_blk, value_blk, visible, nearby = key_slice(block_index)

        def output_accumulate(state_now):
            scores = block_scores(query_b, key_blk)
            probs_b = jnp.exp(jnp.where(visible, scores - log_sum[..., None], NEG_LARGE)).astype(
                NARROW_TYPE
            )
            return state_now + jnp.einsum(
                "rhqk,rkhd->rqhd", probs_b, value_blk, preferred_element_type=WIDE_TYPE
            )

        return (lax.cond(nearby, output_accumulate, unchanged, running), None)

    attn_out, unused = lax.scan(
        output_step,
        jnp.zeros((rows_n, group_len, heads_here, HD), WIDE_TYPE),
        jnp.arange(block_count, dtype=jnp.int32),
    )
    attn_b = attn_out.astype(NARROW_TYPE).reshape(token_count, local_width)
    a_out_f = adapt_a_out.astype(WIDE_TYPE)
    b_out_f = adapt_b_out.astype(WIDE_TYPE)
    out_full = base_out.astype(WIDE_TYPE) + ADAPT_SCALE * jnp.dot(
        a_out_f, b_out_f, precision=FULL_PRECISION
    )
    out_pre_sum, out_low_sum, out_squares = (
        lax.psum(
            jnp.dot(attn_b, base_out, preferred_element_type=WIDE_TYPE).astype(jnp.bfloat16),
            "heads",
        ).astype(jnp.float32),
        lax.psum(
            jnp.dot(attn_b, adapt_a_out, preferred_element_type=WIDE_TYPE).astype(jnp.bfloat16),
            "heads",
        ).astype(jnp.float32),
        lax.psum(jnp.sum(out_full * out_full, axis=0).astype(jnp.bfloat16), "heads").astype(
            jnp.float32
        ),
    )
    out_low = out_low_sum.astype(NARROW_TYPE)
    out_pre = out_pre_sum + ADAPT_SCALE * jnp.dot(
        out_low, adapt_b_out, preferred_element_type=WIDE_TYPE
    )
    out_norm = jnp.sqrt(out_squares + COLUMN_EPS)
    out_scale = magnitude_out / out_norm
    residual = inputs + out_pre * out_scale
    inverse_two = lax.rsqrt(jnp.mean(residual * residual, axis=-1, keepdims=True) + NORM_EPS)
    normed_two = (residual * inverse_two * ffn_gain).astype(NARROW_TYPE)
    gate_pre, gate_low, gate_norm, gate_full = project_columns(
        normed_two, base_gu[0], adapt_a_gu[0], adapt_b_gu[0]
    )
    up_pre, up_low, up_norm, up_full = project_columns(
        normed_two, base_gu[1], adapt_a_gu[1], adapt_b_gu[1]
    )
    gate_scale = magnitude_gu[0] / gate_norm
    up_scale = magnitude_gu[1] / up_norm
    gate_act = gate_pre * gate_scale
    up_act = up_pre * up_scale
    hidden_b = (jax.nn.silu(gate_act) * up_act).astype(NARROW_TYPE)
    a_down_f = adapt_a_down.astype(WIDE_TYPE)
    b_down_f = adapt_b_down.astype(WIDE_TYPE)
    down_full = base_down.astype(WIDE_TYPE) + ADAPT_SCALE * jnp.dot(
        a_down_f, b_down_f, precision=FULL_PRECISION
    )
    down_pre_sum, down_low_sum, down_squares = (
        lax.psum(
            jnp.dot(hidden_b, base_down, preferred_element_type=WIDE_TYPE).astype(jnp.bfloat16),
            "heads",
        ).astype(jnp.float32),
        lax.psum(
            jnp.dot(hidden_b, adapt_a_down, preferred_element_type=WIDE_TYPE).astype(jnp.bfloat16),
            "heads",
        ).astype(jnp.float32),
        lax.psum(jnp.sum(down_full * down_full, axis=0).astype(jnp.bfloat16), "heads").astype(
            jnp.float32
        ),
    )
    down_low = down_low_sum.astype(NARROW_TYPE)
    down_pre = down_pre_sum + ADAPT_SCALE * jnp.dot(
        down_low, adapt_b_down, preferred_element_type=WIDE_TYPE
    )
    down_norm = jnp.sqrt(down_squares + COLUMN_EPS)
    down_scale = magnitude_down / down_norm
    mixed = (
        (residual + down_pre * down_scale)
        .astype(NARROW_TYPE)
        .reshape(rows_n, group_len, model_width)
    )
    grad_y = cotangent.astype(WIDE_TYPE).reshape(token_count, model_width)
    down_sums = jnp.sum(grad_y * down_pre, axis=0)
    down_grad_pre = (grad_y * down_scale).astype(NARROW_TYPE)
    down_grad_b = ADAPT_SCALE * jnp.einsum(
        "tr,tc->rc", down_low, down_grad_pre, preferred_element_type=WIDE_TYPE
    )
    down_d_low = ADAPT_SCALE * jnp.einsum(
        "tc,rc->tr", down_grad_pre, adapt_b_down, preferred_element_type=WIDE_TYPE
    )
    grad_hidden = jnp.einsum(
        "tc,fc->tf", down_grad_pre, base_down, preferred_element_type=WIDE_TYPE
    ) + jnp.dot(down_d_low, a_down_f.T, precision=FULL_PRECISION)
    down_grad_a = jnp.einsum(
        "tf,tr->fr", hidden_b.astype(WIDE_TYPE), down_d_low, precision=FULL_PRECISION
    )
    sigmoid_g = jax.nn.sigmoid(gate_act)
    grad_gate = grad_hidden * up_act * sigmoid_g * (1.0 + gate_act * (1.0 - sigmoid_g))
    grad_up = grad_hidden * gate_act * sigmoid_g
    gate_sums, gate_input, gate_d_low, gate_grad_b, unused = column_back(
        grad_gate, gate_pre, gate_scale, gate_low, base_gu[0], adapt_b_gu[0]
    )
    up_sums, up_input, up_d_low, up_grad_b, unused = column_back(
        grad_up, up_pre, up_scale, up_low, base_gu[1], adapt_b_gu[1]
    )
    down_total, gate_total, up_total = lax.psum((down_sums, gate_sums, up_sums), "seq")
    a_gu_f = adapt_a_gu.astype(WIDE_TYPE)
    b_gu_f = adapt_b_gu.astype(WIDE_TYPE)
    down_norm_a, down_norm_b, down_grad_m = norm_path(
        down_full, a_down_f, b_down_f, magnitude_down, down_norm, down_total
    )
    gate_norm_a, gate_norm_b, gate_grad_m = norm_path(
        gate_full, a_gu_f[0], b_gu_f[0], magnitude_gu[0], gate_norm, gate_total
    )
    up_norm_a, up_norm_b, up_grad_m = norm_path(
        up_full, a_gu_f[1], b_gu_f[1], magnitude_gu[1], up_norm, up_total
    )
    ffn_input, ffn_low, gu_norm_a, down_norm_b_sum = (
        lax.psum((gate_input + up_input).astype(jnp.bfloat16), "heads").astype(jnp.float32),
        lax.psum(jnp.stack([gate_d_low, up_d_low]).astype(jnp.bfloat16), "heads").astype(
            jnp.float32
        ),
        lax.psum(jnp.stack([gate_norm_a, up_norm_a]).astype(jnp.bfloat16), "heads").astype(
            jnp.float32
        ),
        lax.psum(down_norm_b.astype(jnp.bfloat16), "heads").astype(jnp.float32),
    )
    grad_normed_two = (
        ffn_input
        + jnp.dot(ffn_low[0], a_gu_f[0].T, precision=FULL_PRECISION)
        + jnp.dot(ffn_low[1], a_gu_f[1].T, precision=FULL_PRECISION)
    )
    gu_grad_a = jnp.einsum(
        "ti,str->sir", normed_two.astype(WIDE_TYPE), ffn_low, precision=FULL_PRECISION
    )
    grad_back_two, ffn_gain_grad = rms_back(residual, inverse_two, ffn_gain, grad_normed_two)
    grad_residual = grad_y + grad_back_two
    out_sums = jnp.sum(grad_residual * out_pre, axis=0)
    out_grad_pre = (grad_residual * out_scale).astype(NARROW_TYPE)
    out_grad_b = ADAPT_SCALE * jnp.einsum(
        "tr,tc->rc", out_low, out_grad_pre, preferred_element_type=WIDE_TYPE
    )
    out_d_low = ADAPT_SCALE * jnp.einsum(
        "tc,rc->tr", out_grad_pre, adapt_b_out, preferred_element_type=WIDE_TYPE
    )
    grad_attn = (
        jnp.einsum("tc,lc->tl", out_grad_pre, base_out, preferred_element_type=WIDE_TYPE)
        + jnp.dot(out_d_low, a_out_f.T, precision=FULL_PRECISION)
    ).astype(NARROW_TYPE)
    out_grad_a = jnp.einsum(
        "tl,tr->lr", attn_b.astype(WIDE_TYPE), out_d_low, precision=FULL_PRECISION
    )
    grad_attn4 = grad_attn.reshape(rows_n, group_len, heads_here, HD)
    delta_row = jnp.sum(grad_attn4.astype(WIDE_TYPE) * attn_out, axis=3).transpose(0, 2, 1)

    def back_step(running, block_index):
        key_blk, value_blk, visible, nearby = key_slice(block_index)

        def back_accumulate(state_now):
            probs_b, grad_scores = block_grads(
                query_b, key_blk, value_blk, grad_attn4, log_sum, delta_row, visible
            )
            grad_q = (
                state_now[0]
                + jnp.einsum(
                    "rhqk,rkhd->rqhd", grad_scores, key_blk, preferred_element_type=WIDE_TYPE
                )
                * key_scale
            )
            grad_k = (
                jnp.einsum(
                    "rhqk,rqhd->rkhd", grad_scores, query_b, preferred_element_type=WIDE_TYPE
                )
                * key_scale
            )
            grad_v = jnp.einsum(
                "rhqk,rqhd->rkhd", probs_b, grad_attn4, preferred_element_type=WIDE_TYPE
            )
            joined = jnp.concatenate(
                [
                    grad_k.reshape(rows_n, key_block, local_width),
                    grad_v.reshape(rows_n, key_block, local_width),
                ],
                axis=2,
            )
            return (
                grad_q,
                lax.dynamic_update_slice_in_dim(state_now[1], joined, block_index * key_block, 1),
            )

        return (lax.cond(nearby, back_accumulate, unchanged, running), None)

    start_state = (
        jnp.zeros((rows_n, group_len, heads_here, HD), WIDE_TYPE),
        jnp.zeros((rows_n, row_len, 2 * local_width), WIDE_TYPE),
    )
    result, unused_out = lax.scan(back_step, start_state, jnp.arange(block_count, dtype=jnp.int32))
    grad_query, terms = result
    key_value_grads = lax.psum_scatter(
        terms.astype(jnp.bfloat16), "seq", scatter_dimension=1, tiled=True
    ).astype(jnp.float32)
    grad_key4 = key_value_grads[:, :, :local_width].reshape(rows_n, group_len, heads_here, HD)
    grad_value4 = key_value_grads[:, :, local_width:].reshape(rows_n, group_len, heads_here, HD)
    grad_shaped = [
        rotate_back(grad_query, cosine, sine_t).reshape(token_count, local_width),
        rotate_back(grad_key4, cosine, sine_t).reshape(token_count, local_width),
        grad_value4.reshape(token_count, local_width),
    ]
    qkv_back = [
        column_back(
            grad_shaped[slot_at],
            qkv_parts[slot_at][0],
            qkv_scale[slot_at],
            qkv_parts[slot_at][1],
            base_qkv[slot_at],
            adapt_b_qkv[slot_at],
        )
        for slot_at in range(3)
    ]
    out_total, qkv_total = lax.psum(
        (out_sums, jnp.stack([qkv_back[slot_at][0] for slot_at in range(3)])), "seq"
    )
    a_qkv_f = adapt_a_qkv.astype(WIDE_TYPE)
    b_qkv_f = adapt_b_qkv.astype(WIDE_TYPE)
    out_norm_a, out_norm_b, out_grad_m = norm_path(
        out_full, a_out_f, b_out_f, magnitude_out, out_norm, out_total
    )
    qkv_norm = [
        norm_path(
            qkv_parts[slot_at][3],
            a_qkv_f[slot_at],
            b_qkv_f[slot_at],
            magnitude_qkv[slot_at],
            qkv_parts[slot_at][2],
            qkv_total[slot_at],
        )
        for slot_at in range(3)
    ]
    attn_input, qkv_low, qkv_norm_a, out_norm_b_sum = (
        lax.psum(
            (qkv_back[0][1] + qkv_back[1][1] + qkv_back[2][1]).astype(jnp.bfloat16), "heads"
        ).astype(jnp.float32),
        lax.psum(
            jnp.stack([qkv_back[slot_at][2] for slot_at in range(3)]).astype(jnp.bfloat16), "heads"
        ).astype(jnp.float32),
        lax.psum(
            jnp.stack([qkv_norm[slot_at][0] for slot_at in range(3)]).astype(jnp.bfloat16), "heads"
        ).astype(jnp.float32),
        lax.psum(out_norm_b.astype(jnp.bfloat16), "heads").astype(jnp.float32),
    )
    grad_normed = (
        attn_input
        + jnp.dot(qkv_low[0], a_qkv_f[0].T, precision=FULL_PRECISION)
        + jnp.dot(qkv_low[1], a_qkv_f[1].T, precision=FULL_PRECISION)
        + jnp.dot(qkv_low[2], a_qkv_f[2].T, precision=FULL_PRECISION)
    )
    qkv_grad_a = jnp.einsum(
        "ti,str->sir", normed_b.astype(WIDE_TYPE), qkv_low, precision=FULL_PRECISION
    )
    grad_back_one, attn_gain_grad = rms_back(inputs, inverse_one, attn_gain, grad_normed)
    grad_tokens = (grad_residual + grad_back_one).reshape(rows_n, group_len, model_width)
    summed = (
        lax.psum(qkv_grad_a.astype(jnp.bfloat16), "seq").astype(jnp.float32),
        lax.psum(
            jnp.stack([qkv_back[slot_at][3] for slot_at in range(3)]).astype(jnp.bfloat16), "seq"
        ).astype(jnp.float32),
        lax.psum(out_grad_a.astype(jnp.bfloat16), "seq").astype(jnp.float32),
        lax.psum(out_grad_b.astype(jnp.bfloat16), "seq").astype(jnp.float32),
        lax.psum(gu_grad_a.astype(jnp.bfloat16), "seq").astype(jnp.float32),
        lax.psum(jnp.stack([gate_grad_b, up_grad_b]).astype(jnp.bfloat16), "seq").astype(
            jnp.float32
        ),
        lax.psum(down_grad_a.astype(jnp.bfloat16), "seq").astype(jnp.float32),
        lax.psum(down_grad_b.astype(jnp.bfloat16), "seq").astype(jnp.float32),
        lax.psum(attn_gain_grad.astype(jnp.bfloat16), "seq").astype(jnp.float32),
        lax.psum(ffn_gain_grad.astype(jnp.bfloat16), "seq").astype(jnp.float32),
    )
    grad_a_qkv = summed[0] + qkv_norm_a
    grad_b_qkv = summed[1] + jnp.stack([qkv_norm[slot_at][1] for slot_at in range(3)])
    grad_m_qkv = jnp.stack([qkv_norm[slot_at][2] for slot_at in range(3)])
    grad_a_out = summed[2] + out_norm_a
    grad_b_out = summed[3] + out_norm_b_sum
    grad_a_gu = summed[4] + gu_norm_a
    grad_b_gu = summed[5] + jnp.stack([gate_norm_b, up_norm_b])
    grad_m_gu = jnp.stack([gate_grad_m, up_grad_m])
    grad_a_down = summed[6] + down_norm_a
    grad_b_down = summed[7] + down_norm_b_sum
    return (
        mixed,
        grad_tokens,
        summed[8],
        grad_a_qkv,
        grad_b_qkv,
        grad_m_qkv,
        grad_a_out,
        grad_b_out,
        out_grad_m,
        summed[9],
        grad_a_gu,
        grad_b_gu,
        grad_m_gu,
        grad_a_down,
        grad_b_down,
        down_grad_m,
    )


def solution(mesh):
    in_specs = (
        P(None, "seq", None),
        P(),
        P(None, None, "heads"),
        P(),
        P(None, None, "heads"),
        P(None, "heads"),
        P("heads", None),
        P("heads", None),
        P(),
        P(),
        P(),
        P(None, None, "heads"),
        P(),
        P(None, None, "heads"),
        P(None, "heads"),
        P("heads", None),
        P("heads", None),
        P(),
        P(),
        P(),
        P(None, "seq", None),
    )
    out_specs = (
        P(None, "seq", None),
        P(None, "seq", None),
        P(),
        P(),
        P(None, None, "heads"),
        P(None, "heads"),
        P("heads", None),
        P(),
        P(),
        P(),
        P(),
        P(None, None, "heads"),
        P(None, "heads"),
        P("heads", None),
        P(),
        P(),
    )
    return jax.shard_map(
        per_device, mesh=mesh, in_specs=in_specs, out_specs=out_specs, check_vma=False
    )
```

profile of v0, /device:TPU:0, one launch (start us, length us, event | category | flops | bytes accessed | tf_op | source)
XLA Modules:
  0.0 984.9 jit_solution(14081640993691508431)
XLA Ops:
  17.1 3.0 multiply_reduce_fusion.10
  20.2 2.9 multiply_reduce_fusion.9
  23.1 2.9 multiply_reduce_fusion.8
  38.0 2.9 broadcast_multiply_fusion
  52.0 2.9 fusion.188
  58.1 7.2 multiply_reduce_fusion.2
  66.0 7.6 multiply_reduce_fusion.1
  74.3 2.9 multiply_reduce_fusion.7
  77.2 5.4 multiply_reduce_fusion
  82.6 8.9 all-gather.3.cloned.1.call-done
  91.6 15.3 %while.55 = (s32[]{:T(128)}, f32[2,4,256]{2,1,0:T(4,128)S(1)}, f32[2,4,256]{2,1,0:T(4,128)S(1)}, s32[4]{0:T(128)S(1)}, s32[]{:T(128)}, /*index=5*/s32[]{:T(128)}...) while((s32[]{:T(128)}, f32[2,4,256]{2,1,0:T(4,128)S(1)}, ...), condition=%wide.region_16.17_spmd.clone, body=%wide.region_7.16_spmd.clone.sunk | while | flops 277639264 | bytes 13041173 | solution.py:230
  94.3 4.1 conditional.9
  106.9 24.0 %all-gather.5.cloned.1.call-done = bf16[2,2048,512]{1,2,0:T(8,128)(2,1)} async-done(((bf16[2,256,512]{1,2,0:T(8,128)(2,1)}), bf16[2,2048,512]{1,2,0:T(8,128)(2,1)}) %all-gather.5.cloned.1.call-update) | async-done | bytes 4194320 | tf_op jit(solution)/shard_map/all_gather | solution.py:189
  132.0 18.5 %while.56 = (s32[]{:T(128)}, f32[2,256,4,128]{3,1,2,0:T(8,128)}, s32[4]{0:T(128)S(1)}, s32[]{:T(128)}, s32[]{:T(128)}, /*index=5*/s32[2,8]{1,0:T(2,128)S(1)}, s3...) while((s32[]{:T(128)}, f32[2,256,4,128]{3,1,2,0:T(8,128)}, ...), condition=%wide.region_24.25_spmd.clone, body=%wide.region_17.24_spmd.clone.sunk | while | flops 542138496 | bytes 9534981 | solution.py:249
  134.8 7.2 conditional.10
  135.1 2.7 constant_dynamic-slice_fusion.1
  137.9 4.2 fusion.11
  152.6 4.3 convolution_convert_fusion
  157.0 19.0 %all-reduce.4 = (bf16[512,16]{0,1:T(8,128)(2,1)S(1)}, bf16[2048]{0:T(1024)(128)(2,1)S(1)}, bf16[2048]{0:T(1024)(128)(2,1)S(1)}) all-reduce(bf16[512,16]{0,1:T(8,128)(2,1)S(1)} %convolution_convert_fusion.12, bf16[2048]{0:T(1024)(128)(2,1)S(1)} %get-tuple-element.1678, ...), channel_id=1, replica_groups=mesh['seq'=8,'heads'=4] {'heads'}, use_global_device_ids=true, to_apply=%region_26.27 | all-reduce | flops 12288 | bytes 49152 | tf_op jit(solution)/shard_map/psum | solution.py:265
  177.3 5.9 fusion.381
  183.2 3.1 convolution_add_fusion
  186.3 79.4 %all-reduce.14.cloned.1.call-done = bf16[512,2048]{1,0:T(8,128)(2,1)} async-done(((bf16[512,2048]{1,0:T(8,128)(2,1)}), bf16[512,2048]{1,0:T(8,128)(2,1)}) %all-reduce.14.cloned.1.call-update) | async-done | bytes 2097168 | tf_op jit(solution)/shard_map/psum | solution.py:261
  265.7 5.0 multiply_reduce_fusion.6
  274.8 3.4 fusion.47
  278.2 3.4 fusion.51
  282.3 3.1 multiply_reduce_fusion.12
  285.4 4.8 convolution_convert_fusion.1
  290.4 3.4 fusion.45
  293.8 4.7 add_convert_fusion.1
  299.6 17.8 %psum.210 = bf16[2,512,16]{1,2,0:T(8,128)(2,1)S(1)} all-reduce(bf16[2,512,16]{1,2,0:T(8,128)(2,1)S(1)} %pad_maximum_fusion.9), channel_id=1, replica_groups=mesh['seq'=8,'heads'=4] {'heads'}, use_global_device_ids=true, to_apply=%region_37.38 | all-reduce | flops 16384 | bytes 65536 | tf_op jit(solution)/shard_map/psum | solution.py:360
  317.5 2.8 fusion.285
  320.3 133.4 %all-reduce.24.cloned.1.call-done = (bf16[512,2048]{1,0:T(8,128)(2,1)}, bf16[512,2048]{1,0:T(8,128)(2,1)}) async-done(((bf16[512,2048]{1,0:T(8,128)(2,1)}, bf16[512,2048]{1,0:T(8,128)(2,1)}), (bf16[512,2048]{1,0:T(8,128)(2,1)}, bf16[512,2048]{1,0:T(8,128)(2,1)})) %all-reduce.24.cloned.1.call-update) | async-done | bytes 4194320 | tf_op jit(solution)/shard_map/psum | solution.py:299
  453.7 6.3 multiply_reduce_fusion.3
  470.6 4.4 broadcast_in_dim.95
  475.0 22.9 %while.57 = (s32[]{:T(128)}, f32[2,256,4,128]{3,1,2,0:T(8,128)S(1)}, bf16[2,2048,1024]{1,2,0:T(8,128)(2,1)}, s32[4]{0:T(128)S(1)}, s32[]{:T(128)}, /*index=5*/s3...) while((s32[]{:T(128)}, ...), condition=%wide.region_47.48_spmd.clone, body=%wide.region_40.0_spmd.clone.sunk | while | flops 1359241344 | bytes 37600912 | solution.py:437
  478.3 11.0 %conditional.11 = ((f32[2,256,4,128]{3,1,2,0:T(8,128)S(1)}, bf16[2,2048,1024]{1,2,0:T(8,128)(2,1)})) conditional(s32[]{:T(128)} %convert_element_type.714, (f32[2,256,4,128]{3,1,2,0:T(8,128)S(1)}, bf16[2,2048,1024]{1,2,0:T(8,128)(2,1)}) %tuple.273, (s32[2,256]{1,0:T(2,128)S(1)}, s32[2,512,8]{2,1,0:T(8,128)S(1)}, s32[]{:T(128)}, s32[512]{0:T(512)S(1)}, ...), branch_computations={%region_44.44_spmd, %region_45.46_spmd} | conditional | flops 1359224320 | bytes 37561464 | solution.py:431
  479.5 2.7 constant_dynamic-slice_fusion.3
  497.9 11.9 %copy.139 = bf16[2,2048,1024]{2,1,0:T(8,128)(2,1)} copy(bf16[2,2048,1024]{1,2,0:T(8,128)(2,1)} %get-tuple-element.1239) | data formatting | bytes 16777216 | tf_op jit(solution)/shard_map/while | solution.py:437
  524.0 89.0 %reduce-scatter.2.cloned.1.call-done = bf16[2,256,1024]{2,1,0:T(8,128)(2,1)} async-done(((bf16[2,2048,1024]{2,1,0:T(8,128)(2,1)}), bf16[2,256,1024]{2,1,0:T(8,128)(2,1)}) %reduce-scatter.2.cloned.1.call-update) | async-done | bytes 1048592 | tf_op jit(solution)/shard_map/reduce_scatter | solution.py:439
  619.0 4.9 fusion.194
  626.1 5.0 fusion.190
  639.0 6.8 add_convert_fusion
  646.4 26.7 %all-reduce.20.cloned.1.call-done = (bf16[512,16]{0,1:T(8,128)(2,1)}, bf16[3,512,16]{1,2,0:T(8,128)(2,1)}) async-done(((bf16[512,16]{0,1:T(8,128)(2,1)}, bf16[3,512,16]{1,2,0:T(8,128)(2,1)}), (bf16[512,16]{0,1:T(8,128)(2,1)}, bf16[3,512,16]{1,2,0:T(8,128)(2,1)})) %all-reduce.20.cloned.1.call-update) | async-done | bytes 65552 | tf_op jit(solution)/shard_map/psum | solution.py:303
  673.3 5.7 fusion.64
  679.0 23.0 %all-reduce = (f32[3,512]{1,0:T(4,128)S(1)}, f32[2048]{0:T(1024)S(1)}, f32[1408]{0:T(1024)S(1)}, f32[1408]{0:T(1024)S(1)}, f32[2048]{0:T(1024)S(1)}) all-reduce(f32[3,512]{1,0:T(4,128)S(1)} %pad_maximum_fusion.11, f32[2048]{0:T(1024)S(1)} %copy-done.75, f32[1408]{0:T(1024)S(1)} %copy-done.107, ...), channel_id=1, replica_groups=mesh['seq'=8,'heads'=4] {'seq'}, use_global_device_ids=true, to_apply=%region_58.59 | all-reduce | flops 8448 | bytes 67584 | tf_op jit(solution)/shard_map/psum | solution.py:460
  702.1 3.9 fusion.225
  708.2 3.9 fusion.231
  712.2 4.3 fusion.168
  719.3 10.2 %fusion.182 = bf16[16,2048]{1,0:T(8,128)(2,1)} fusion(bf16[1408,16]{0,1:T(8,128)(2,1)S(1)} %copy-done.47, f32[1408,2048]{1,0:T(8,128)} %get-tuple-element.1681, f32[2048]{0:T(1024)S(1)} %get-tuple-element.1642), kind=kOutput, calls=%fused_computation.216 | convolution fusion | flops 556597248 | bytes 11653120 | tf_op jit(solution)/shard_map/dot_general | solution.py:126
  732.0 5.7 fusion.179
  737.8 5.9 fusion.176
  746.4 3.7 fusion.219
  751.2 2.8 fusion.299
  753.9 2.8 fusion.294
  756.8 8.5 fusion.119
  765.3 4.2 fusion.113
  769.5 78.0 %all-reduce.22.cloned.1.call-done = (bf16[512,2048]{1,0:T(8,128)(2,1)}, bf16[3,2048,16]{1,2,0:T(8,128)(2,1)}, bf16[16,2048]{1,0:T(8,128)(2,1)}, bf16[2,2048,16]{1,2,0:T(8,128)(2,1)}, bf16[16,2048]{1,0:T(8,128)(2,1)}) async-done(((bf16[512,2048]{1,0:T(8,128)(2,1)}, bf16[3,2048,16]{1,2,0:T(8,128)(2,1)}, bf16[16,2048]{1,0:T(8,128)(2,1)}, bf16[2,2048,16]{1,2,0:T(8,128)(2,1)}, bf16[16,2048]{1,0:T(8,128)(2,1)}), ...) | async-done | bytes 2555920 | tf_op jit(solution)/shard_map/psum | solution.py:480
  847.5 7.0 fusion.73
  854.5 3.1 fusion.70
  857.6 2.7 fusion.96
  860.4 49.4 %all-reduce.16.cloned.1.call-done = (bf16[2048]{0:T(1024)(128)(2,1)}, bf16[3,16,512]{2,1,0:T(8,128)(2,1)}, bf16[512,16]{0,1:T(8,128)(2,1)}, bf16[2048]{0:T(1024)(128)(2,1)}, bf16[1408,16]{0,1:T(8,128)(2,1)}) async-done(((bf16[2048]{0:T(1024)(128)(2,1)}, bf16[3,16,512]{2,1,0:T(8,128)(2,1)}, bf16[512,16]{0,1:T(8,128)(2,1)}, bf16[2048]{0:T(1024)(128)(2,1)}, bf16[1408,16]{0,1:T(8,128)(2,1)}), ...) | async-done | bytes 118800 | tf_op jit(solution)/shard_map/psum | solution.py:515
  909.9 8.9 fusion.125
  918.9 2.8 fusion.237
  923.5 46.7 %all-reduce.18.cloned.1.call-done = (bf16[3,2048,16]{1,2,0:T(8,128)(2,1)}, bf16[16,2048]{1,0:T(8,128)(2,1)}, bf16[2,2048,16]{1,2,0:T(8,128)(2,1)}, bf16[2,16,1408]{2,1,0:T(8,128)(2,1)}, bf16[16,2048]{1,0:T(8,128)(2,1)}) async-done(((bf16[3,2048,16]{1,2,0:T(8,128)(2,1)}, bf16[16,2048]{1,0:T(8,128)(2,1)}, bf16[2,2048,16]{1,2,0:T(8,128)(2,1)}, bf16[2,16,1408]{2,1,0:T(8,128)(2,1)}, bf16[16,2048]{1,0:T(8,128)(2,1)}), ...) | async-done | bytes 548880 | tf_op jit(solution)/shard_map/psum | solution.py:503
  (514 shorter events, 139.7 us)
Async XLA Ops:
  7.2 70.0 %copy-start = (bf16[16,2048]{1,0:T(8,128)(2,1)S(1)}, bf16[16,2048]{1,0:T(8,128)(2,1)}, u32[]{:S(2)}) copy-start(bf16[16,2048]{1,0:T(8,128)(2,1)} %param.50) | copy-start | bytes 196612
  7.2 84.3 %all-gather.3.cloned.1.call-start = ((), (), s32[]{:S(2)}) async-start(), calls=%async_computation.1 | async-start | bytes 4718592 | tf_op jit(solution)/shard_map/all_gather | solution.py:188
  12.9 25.1 %copy-start.56 = (bf16[512,16]{0,1:T(8,128)(2,1)}, bf16[512,16]{0,1:T(8,128)(2,1)S(1)}, u32[]{:S(2)}) copy-start(bf16[512,16]{0,1:T(8,128)(2,1)S(1)} %convolution_convert_fusion.9) | copy-start | bytes 49156
  13.6 14.5 %copy-start.54 = (bf16[512,16]{0,1:T(8,128)(2,1)}, bf16[512,16]{0,1:T(8,128)(2,1)S(1)}, u32[]{:S(2)}) copy-start(bf16[512,16]{0,1:T(8,128)(2,1)S(1)} %convolution_convert_fusion.10) | copy-start | bytes 49156
  28.1 9.9 %copy-start.87 = (f32[1,512]{1,0:T(1,128)}, f32[1,512]{1,0:T(1,128)S(1)}, u32[]{:S(2)}) copy-start(f32[1,512]{1,0:T(1,128)S(1)} %get-tuple-element.1653) | copy-start | bytes 6148
  28.1 26.8 %copy-start.73 = (f32[1,512]{1,0:T(1,128)}, f32[1,512]{1,0:T(1,128)S(1)}, u32[]{:S(2)}) copy-start(f32[1,512]{1,0:T(1,128)S(1)} %get-tuple-element.1651) | copy-start | bytes 6148
  51.3 79.7 %all-gather.5.cloned.1.call-start = ((), (), s32[]{:S(2)}) async-start(), calls=%async_computation.2 | async-start | bytes 4718592 | tf_op jit(solution)/shard_map/all_gather | solution.py:189
  57.2 208.4 %all-reduce.14.cloned.1.call-start = ((), (), s32[]{:S(2)}) async-start(), calls=%async_computation.3 | async-start | bytes 4194304 | tf_op jit(solution)/shard_map/psum | solution.py:261
  65.4 11.8 %slice-start.12 = ((s8[5767168]{0:T(1024)(128)(4,1)}), s8[4194304]{0:T(1024)(128)(4,1)S(1)}, s32[]{:S(2)}) async-start(s8[5767168]{0:T(1024)(128)(4,1)} %bitcast.515), calls=%async_computation.22 | async-start | bytes 8388608
  66.0 8.3 copy-start.36
  66.0 8.3 copy-start.43
  66.0 8.3 copy-start.52
  66.0 11.2 %slice-start.13 = ((s8[5767168]{0:T(1024)(128)(4,1)}), s8[1572864]{0:T(1024)(128)(4,1)S(1)}, s32[]{:S(2)}) async-start(s8[5767168]{0:T(1024)(128)(4,1)} %bitcast.515), calls=%async_computation.23 | async-start | bytes 3145728
  73.6 9.0 copy-start.67
  152.5 23.4 %copy-start.78 = (f32[2048]{0:T(1024)S(1)}, f32[2048]{0:T(1024)}, u32[]{:S(2)}) copy-start(f32[2048]{0:T(1024)} %param.42) | copy-start | bytes 24580
  152.5 23.4 %copy-start.80 = (f32[2048]{0:T(1024)S(1)}, f32[2048]{0:T(1024)}, u32[]{:S(2)}) copy-start(f32[2048]{0:T(1024)} %param.51) | copy-start | bytes 24580
  152.5 23.5 %copy-start.16 = (bf16[2,256,2048]{2,1,0:T(8,128)(2,1)S(1)}, bf16[2,256,2048]{2,1,0:T(8,128)(2,1)}, u32[]{:S(2)}) copy-start(bf16[2,256,2048]{2,1,0:T(8,128)(2,1)} %param.53) | copy-start | bytes 6291460
  156.9 296.8 %all-reduce.24.cloned.1.call-start = ((), (), s32[]{:S(2)}) async-start(), calls=%async_computation.9 | async-start | bytes 8388608 | tf_op jit(solution)/shard_map/psum | solution.py:299
  183.2 82.5 %copy-start.5 = (bf16[2,256,2048]{2,1,0:T(8,128)(2,1)S(1)}, bf16[2,256,2048]{2,1,0:T(8,128)(2,1)}, u32[]{:S(2)}) copy-start(bf16[2,256,2048]{2,1,0:T(8,128)(2,1)} %param.33) | copy-start | bytes 6291460
  265.7 7.8 slice-start.10
  285.4 13.2 %copy-start.27 = (bf16[512,1408]{1,0:T(8,128)(2,1)}, bf16[512,1408]{1,0:T(8,128)(2,1)S(1)}, u32[]{:S(2)}) copy-start(bf16[512,1408]{1,0:T(8,128)(2,1)S(1)} %get-tuple-element.1606) | copy-start | bytes 4325380
  290.4 8.7 copy-start.23
  298.6 314.4 %reduce-scatter.2.cloned.1.call-start = ((), (), s32[]{:S(2)}) async-start(), calls=%async_computation.4 | async-start | bytes 9437184 | tf_op jit(solution)/shard_map/reduce_scatter | solution.py:439
  509.8 163.3 %all-reduce.20.cloned.1.call-start = ((), (), s32[]{:S(2)}) async-start(), calls=%async_computation.7 | async-start | bytes 131072 | tf_op jit(solution)/shard_map/psum | solution.py:303
  510.0 8.9 copy-start.14
  510.5 9.6 copy-start.76
  521.3 94.5 %copy-start.39 = (f32[2,256,64]{1,2,0:T(8,128)S(1)}, f32[2,256,64]{1,2,0:T(8,128)}, u32[]{:S(2)}) copy-start(f32[2,256,64]{1,2,0:T(8,128)} %copy-done.38) | copy-start | bytes 393220
  639.0 34.2 %copy-start.18 = (bf16[2,256,2048]{2,1,0:T(8,128)(2,1)S(1)}, bf16[2,256,2048]{2,1,0:T(8,128)(2,1)}, u32[]{:S(2)}) copy-start(bf16[2,256,2048]{2,1,0:T(8,128)(2,1)} %param.53) | copy-start | bytes 6291460
  639.0 34.2 %copy-start.64 = (f32[2048]{0:T(1024)S(1)}, f32[2048]{0:T(1024)}, u32[]{:S(2)}) copy-start(f32[2048]{0:T(1024)} %copy-done.63) | copy-start | bytes 24580
  639.0 208.5 %all-reduce.22.cloned.1.call-start = ((), (), s32[]{:S(2)}) async-start(), calls=%async_computation.8 | async-start | bytes 5111808 | tf_op jit(solution)/shard_map/psum | solution.py:480
  673.2 28.8 %copy-start.90 = (f32[512]{0:T(512)S(1)}, f32[512]{0:T(512)}, u32[]{:S(2)}) copy-start(f32[512]{0:T(512)} %copy-done.89) | copy-start | bytes 6148
  673.2 28.8 %copy-start.92 = (f32[512]{0:T(512)S(1)}, f32[512]{0:T(512)}, u32[]{:S(2)}) copy-start(f32[512]{0:T(512)} %copy-done.91) | copy-start | bytes 6148
  673.2 28.8 %copy-start.94 = (f32[512]{0:T(512)S(1)}, f32[512]{0:T(512)}, u32[]{:S(2)}) copy-start(f32[512]{0:T(512)} %copy-done.93) | copy-start | bytes 6148
  673.2 28.8 %copy-start.96 = (f32[3,512]{1,0:T(4,128)S(1)}, f32[3,512]{1,0:T(4,128)}, u32[]{:S(2)}) copy-start(f32[3,512]{1,0:T(4,128)} %param.38) | copy-start | bytes 18436
  673.2 28.8 %copy-start.108 = (f32[512]{0:T(512)S(1)}, f32[512]{0:T(512)}, u32[]{:S(2)}) copy-start(f32[512]{0:T(512)} %get-tuple-element.1660) | copy-start | bytes 6148
  673.2 28.8 %copy-start.109 = (f32[512]{0:T(512)S(1)}, f32[512]{0:T(512)}, u32[]{:S(2)}) copy-start(f32[512]{0:T(512)} %get-tuple-element.1658) | copy-start | bytes 6148
  673.2 28.8 %copy-start.110 = (f32[512]{0:T(512)S(1)}, f32[512]{0:T(512)}, u32[]{:S(2)}) copy-start(f32[512]{0:T(512)} %get-tuple-element.1662) | copy-start | bytes 6148
  673.2 28.9 %copy-start.31 = (bf16[3,2048,16]{1,2,0:T(8,128)(2,1)S(1)}, bf16[3,2048,16]{1,2,0:T(8,128)(2,1)}, u32[]{:S(2)}) copy-start(bf16[3,2048,16]{1,2,0:T(8,128)(2,1)} %param.36) | copy-start | bytes 589828
  702.1 29.8 %slice-start.6 = ((s8[11534336]{0:T(1024)(128)(4,1)}), s8[4194304]{0:T(1024)(128)(4,1)S(1)}, s32[]{:S(2)}) async-start(s8[11534336]{0:T(1024)(128)(4,1)} %bitcast.497), calls=%async_computation.16 | async-start | bytes 8388608
  708.2 8.3 copy-start.79
  708.2 8.3 copy-start.81
  708.2 8.3 copy-start.99
  708.2 8.3 copy-start.101
  708.2 8.9 copy-start.7
  708.2 23.7 %slice-start.7 = ((s8[11534336]{0:T(1024)(128)(4,1)}), s8[4194304]{0:T(1024)(128)(4,1)S(1)}, s32[]{:S(2)}) async-start(s8[11534336]{0:T(1024)(128)(4,1)} %bitcast.497), calls=%async_computation.17 | async-start | bytes 8388608
  717.1 12.5 %copy-start.8 = (f32[512,2048]{1,0:T(8,128)S(1)}, f32[512,2048]{1,0:T(8,128)}, u32[]{:S(2)}) copy-start(f32[512,2048]{1,0:T(8,128)} %get-tuple-element.1679) | copy-start | bytes 12582916
  719.3 10.4 %copy-start.53 = (bf16[512,16]{0,1:T(8,128)(2,1)S(1)}, bf16[512,16]{0,1:T(8,128)(2,1)}, u32[]{:S(2)}) copy-start(bf16[512,16]{0,1:T(8,128)(2,1)} %param.40) | copy-start | bytes 49156
  719.3 12.6 %slice-start.8 = ((s8[11534336]{0:T(1024)(128)(4,1)}), s8[3145728]{0:T(1024)(128)(4,1)S(1)}, s32[]{:S(2)}) async-start(s8[11534336]{0:T(1024)(128)(4,1)} %bitcast.497), calls=%async_computation.18 | async-start | bytes 6291456
  719.3 18.4 %slice-start = ((s8[11534336]{0:T(1024)(128)(4,1)}), s8[4194304]{0:T(1024)(128)(4,1)S(1)}, s32[]{:S(2)}) async-start(s8[11534336]{0:T(1024)(128)(4,1)} %bitcast.493), calls=%async_computation.10 | async-start | bytes 8388608
  719.3 18.4 %slice-start.1 = ((s8[11534336]{0:T(1024)(128)(4,1)}), s8[4194304]{0:T(1024)(128)(4,1)S(1)}, s32[]{:S(2)}) async-start(s8[11534336]{0:T(1024)(128)(4,1)} %bitcast.493), calls=%async_computation.11 | async-start | bytes 8388608
  745.1 164.8 %all-reduce.16.cloned.1.call-start = ((), (), s32[]{:S(2)}) async-start(), calls=%async_computation.5 | async-start | bytes 237568 | tf_op jit(solution)/shard_map/psum | solution.py:515
  751.2 14.1 %slice-start.3 = ((s8[11534336]{0:T(1024)(128)(4,1)}), s8[4194304]{0:T(1024)(128)(4,1)S(1)}, s32[]{:S(2)}) async-start(s8[11534336]{0:T(1024)(128)(4,1)} %bitcast.495), calls=%async_computation.13 | async-start | bytes 8388608
  756.8 8.5 slice-start.4
  756.8 8.5 slice-start.5
  765.3 82.2 %copy-start.6 = (bf16[2,256,2048]{2,1,0:T(8,128)(2,1)S(1)}, bf16[2,256,2048]{2,1,0:T(8,128)(2,1)}, u32[]{:S(2)}) copy-start(bf16[2,256,2048]{2,1,0:T(8,128)(2,1)} %param.33) | copy-start | bytes 6291460
  765.3 82.2 %copy-start.62 = (f32[2048]{0:T(1024)S(1)}, f32[2048]{0:T(1024)}, u32[]{:S(2)}) copy-start(f32[2048]{0:T(1024)} %param.34) | copy-start | bytes 24580
  765.3 82.2 %copy-start.77 = (f32[1,2,2,128]{3,1,2,0:T(2,128)S(1)}, f32[1,2,2,128]{3,1,2,0:T(2,128)}, u32[]{:S(2)}) copy-start(f32[1,2,2,128]{3,1,2,0:T(2,128)} %copy-done.76) | copy-start | bytes 6148
  857.6 112.6 %all-reduce.18.cloned.1.call-start = ((), (), s32[]{:S(2)}) async-start(), calls=%async_computation.6 | async-start | bytes 1097728 | tf_op jit(solution)/shard_map/psum | solution.py:503
  909.9 9.0 copy-start.9
  909.9 9.0 copy-start.97
  918.8 51.4 %copy-start.51 = (bf16[3,2048,16]{1,2,0:T(8,128)(2,1)S(1)}, bf16[3,2048,16]{1,2,0:T(8,128)(2,1)}, u32[]{:S(2)}) copy-start(bf16[3,2048,16]{1,2,0:T(8,128)(2,1)} %get-tuple-element.1588) | copy-start | bytes 589828
  918.8 53.1 %copy-start.71 = (bf16[16,2048]{1,0:T(8,128)(2,1)S(1)}, bf16[16,2048]{1,0:T(8,128)(2,1)}, u32[]{:S(2)}) copy-start(bf16[16,2048]{1,0:T(8,128)(2,1)} %get-tuple-element.1589) | copy-start | bytes 196612
  918.8 54.6 %copy-start.70 = (bf16[16,2048]{1,0:T(8,128)(2,1)S(1)}, bf16[16,2048]{1,0:T(8,128)(2,1)}, u32[]{:S(2)}) copy-start(bf16[16,2048]{1,0:T(8,128)(2,1)} %get-tuple-element.1591) | copy-start | bytes 196612
  918.8 56.1 %copy-start.60 = (bf16[2,2048,16]{1,2,0:T(8,128)(2,1)S(1)}, bf16[2,2048,16]{1,2,0:T(8,128)(2,1)}, u32[]{:S(2)}) copy-start(bf16[2,2048,16]{1,2,0:T(8,128)(2,1)} %get-tuple-element.1590) | copy-start | bytes 393220
  (76 other events, 345.9 us)
Sparse Core Ops, SparseCore 0:
  51.4 40.1 all-gather.2
  93.4 37.4 all-gather.4
  157.0 108.5 all-reduce.13
  298.7 154.9 all-reduce.23
  509.9 103.0 reduce-scatter.1
  639.1 34.0 all-reduce.19
  745.2 102.2 all-reduce.21
  857.7 52.0 all-reduce.15
  914.8 55.3 all-reduce.17
where the time goes:
time: 996 us; the launch traced here: 985 us
  waiting for transfers between devices  536 us (54%)
  matrix products  236 us (24%)
  local copies, waits for them, and re-layouts  61.8 us (6%)
  blocking collectives  59.8 us (6%)
  other arithmetic  57.7 us (6%)
  loops' own time  17.3 us (2%)
  between operations  15.7 us (2%)
    psum x1, waiting for transfers between devices, per_device(): lax.psum(jnp.dot(hidden_b, base_down, preferred_element_type=WIDE_TYPE).a...  133 us
    reduce_scatter x1, waiting for transfers between devices, per_device(): lax.psum_scatter(terms.astype(jnp.bfloat16), 'seq', scatter_dimension=1,...  89 us
    psum x1, waiting for transfers between devices, per_device(): lax.psum(jnp.dot(attn_b, base_out, preferred_element_type=WIDE_TYPE).asty...  79.4 us
    psum x1, waiting for transfers between devices, per_device(): lax.psum((qkv_back[0][1] + qkv_back[1][1] + qkv_back[2][1]).astype(jnp.bf...  78 us
    psum x1, waiting for transfers between devices, per_device(): lax.psum(attn_gain_grad.astype(jnp.bfloat16), 'seq').astype(jnp.float32)  49.4 us
    psum x1, waiting for transfers between devices, per_device(): lax.psum(qkv_grad_a.astype(jnp.bfloat16), 'seq').astype(jnp.float32)  46.7 us
    dot_general x7, matrix products, norm_path(): jnp.dot(adapt_a_f.T, weight_grad, precision=FULL_PRECISION)  36.6 us
    dot_general x7, matrix products, norm_path(): jnp.dot(weight_grad, adapt_b_f.T, precision=FULL_PRECISION)  31.9 us
  transfers between devices with their start and end apart: 9, of which 9 were waited for; matrix products, arithmetic and copies ran while one was open for 12% of the time, Pallas kernels for 0%

commit v1 on v0

v1 whole, which is shorter than its diff:
```python
import functools

import jax
import jax.numpy as jnp
from jax import lax
from jax.experimental import pallas as pl
from jax.experimental.pallas import tpu as pltpu
from jax.sharding import PartitionSpec as P

HD = 128
ADAPT_SCALE = 2.0
NORM_EPS = 1e-05
COLUMN_EPS = 1e-06
ROPE_BASE = 10000.0
NEG_LARGE = -1e30
F32 = jnp.float32
BF16 = jnp.bfloat16
MESH = pl.DeviceIdType.MESH
VMEM_LIMIT = 56 * 2**20
NN = (((1,), (0,)), ((), ()))
NT = (((1,), (1,)), ((), ()))
TN = (((0,), (0,)), ((), ()))


def dot(a, b, dims=NN):
    return lax.dot_general(a.astype(BF16), b.astype(BF16), dims, preferred_element_type=F32)


def exchange_plan(kind, me, seq_n, pairs):
    fan = seq_n // pairs
    if kind == "queries":
        return [(p * fan + lax.rem(me, fan), p, me // fan) for p in range(pairs)], seq_n // fan
    if kind == "keys":
        return [(e, e // fan, me) for e in range(seq_n)], seq_n
    if kind == "queries_back":
        return [(lax.rem(me, fan) + fan * i, i, me // fan) for i in range(seq_n // fan)], pairs
    return [(e, e, me) for e in range(seq_n)], seq_n


def exchange_kernel(kinds, seq_n, pairs, *refs):
    n = len(kinds)
    ins, outs, sems = refs[:n], refs[n : 2 * n], refs[2 * n :]
    me = lax.axis_index("seq")
    barrier = pltpu.get_barrier_semaphore()
    for d in range(1, seq_n):
        pl.semaphore_signal(
            barrier, inc=1, device_id={"seq": lax.rem(me + d, seq_n)}, device_id_type=MESH
        )
    pl.semaphore_wait(barrier, seq_n - 1)
    sent, landed = [], []
    for a, kind in enumerate(kinds):
        plan, slots = exchange_plan(kind, me, seq_n, pairs)
        send_sem, recv_sem = sems[2 * a], sems[2 * a + 1]
        for j, (target, block, slot) in enumerate(plan):
            far = pltpu.make_async_remote_copy(
                src_ref=ins[a].at[block],
                dst_ref=outs[a].at[slot],
                send_sem=send_sem.at[j],
                recv_sem=recv_sem.at[slot],
                device_id={"seq": target},
                device_id_type=MESH,
            )
            near = pltpu.make_async_copy(ins[a].at[block], outs[a].at[slot], recv_sem.at[slot])

            @pl.when(target != me)
            def _(far=far):
                far.start()

            @pl.when(target == me)
            def _(near=near):
                near.start()

            sent.append((target, far))
        for slot in range(slots):
            landed.append(
                pltpu.make_async_copy(ins[a].at[0], outs[a].at[slot], recv_sem.at[slot])
            )
    for target, far in sent:

        @pl.when(target != me)
        def _(far=far):
            far.wait_send()

    for near in landed:
        near.wait()


def exchange(kinds, arrays, pairs, collective_id):
    seq_n = lax.axis_size("seq")
    out_shape, scratch = [], []
    for kind, array in zip(kinds, arrays):
        plan, slots = exchange_plan(kind, 0, seq_n, pairs)
        out_shape.append(jax.ShapeDtypeStruct((slots,) + array.shape[1:], array.dtype))
        scratch += [pltpu.SemaphoreType.DMA((len(plan),)), pltpu.SemaphoreType.DMA((slots,))]
    return pl.pallas_call(
        functools.partial(exchange_kernel, kinds, seq_n, pairs),
        out_shape=out_shape,
        in_specs=[pl.BlockSpec(memory_space=pltpu.VMEM)] * len(arrays),
        out_specs=[pl.BlockSpec(memory_space=pltpu.VMEM)] * len(arrays),
        scratch_shapes=scratch,
        compiler_params=pltpu.CompilerParams(
            collective_id=collective_id, has_side_effects=True, vmem_limit_bytes=VMEM_LIMIT
        ),
    )(*arrays)


def line_sum_kernel(depth, chunks, rows, x_ref, out_ref, got, held, *sems):
    up_send, up_recv, down_send, down_recv = sems
    h = lax.axis_index("heads")
    barrier = pltpu.get_barrier_semaphore()
    for step in (-1, 1):

        @pl.when((h + step >= 0) & (h + step < depth))
        def _(step=step):
            pl.semaphore_signal(barrier, inc=1, device_id={"heads": h + step}, device_id_type=MESH)

    pl.semaphore_wait(barrier, jnp.where((h == 0) | (h == depth - 1), 1, 2))

    half = chunks * rows

    def place(stream, c):
        return pl.ds(pl.multiple_of((1 - stream) * half + c * rows, rows), rows)

    def up_copy(stream, c, src, to):
        return pltpu.make_async_remote_copy(
            src_ref=src,
            dst_ref=got.at[stream, c],
            send_sem=up_send.at[stream, c],
            recv_sem=up_recv.at[stream, c],
            device_id={"heads": to},
            device_id_type=MESH,
        )

    def down_copy(stream, c, to):
        return pltpu.make_async_remote_copy(
            src_ref=out_ref.at[place(stream, c)],
            dst_ref=out_ref.at[place(stream, c)],
            send_sem=down_send.at[stream, c],
            recv_sem=down_recv.at[stream, c],
            device_id={"heads": to},
            device_id_type=MESH,
        )

    def step(t, carry):
        for stream in range(2):
            pos = h if stream == 0 else depth - 1 - h
            ahead = h + 1 if stream == 0 else h - 1
            behind = h - 1 if stream == 0 else h + 1
            c = t - pos
            live = (c >= 0) & (c < chunks)

            @pl.when(live & (pos == 0))
            def _():
                up_copy(stream, c, x_ref.at[place(stream, c)], ahead).start()

            @pl.when(live & (pos > 0))
            def _():
                up_copy(stream, c, held.at[stream, c], h).wait_recv()
                total = got[stream, c].astype(F32) + x_ref[place(stream, c), :].astype(F32)

                @pl.when(pos < depth - 1)
                def _():
                    held[stream, c] = total.astype(BF16)
                    up_copy(stream, c, held.at[stream, c], ahead).start()

                @pl.when(pos == depth - 1)
                def _():
                    out_ref[place(stream, c), :] = total.astype(BF16)
                    down_copy(stream, c, behind).start()

            b = t - (2 * (depth - 1) - pos)

            @pl.when((b >= 0) & (b < chunks) & (pos < depth - 1))
            def _():
                down_copy(stream, b, h).wait_recv()

                @pl.when(pos > 0)
                def _():
                    down_copy(stream, b, behind).start()

        return carry

    lax.fori_loop(0, chunks + 2 * (depth - 1), step, 0)

    def drain(c, carry):
        for stream in range(2):
            pos = h if stream == 0 else depth - 1 - h

            @pl.when(pos < depth - 1)
            def _():
                up_copy(stream, c, held.at[stream, c], h).wait_send()

            @pl.when(pos > 0)
            def _():
                down_copy(stream, c, h).wait_send()

        return carry

    lax.fori_loop(0, chunks, drain, 0)


def line_sum(x, collective_id, rows=16):
    depth = lax.axis_size("heads")
    tokens, width = x.shape
    chunks = tokens // (2 * rows)
    sem = pltpu.SemaphoreType.DMA((2, chunks))
    return pl.pallas_call(
        functools.partial(line_sum_kernel, depth, chunks, rows),
        out_shape=jax.ShapeDtypeStruct(x.shape, BF16),
        in_specs=[pl.BlockSpec(memory_space=pltpu.VMEM)],
        out_specs=pl.BlockSpec(memory_space=pltpu.VMEM),
        scratch_shapes=[
            pltpu.VMEM((2, chunks, rows, width), BF16),
            pltpu.VMEM((2, chunks, rows, width), BF16),
            sem,
            sem,
            sem,
            sem,
        ],
        compiler_params=pltpu.CompilerParams(
            collective_id=collective_id, has_side_effects=True, vmem_limit_bytes=VMEM_LIMIT
        ),
    )(x)


def attend_kernel(block, low_ref, high_ref, q_ref, k_ref, v_ref, start_ref, place_ref, o_ref, lse_ref, vt):
    scale = HD**-0.5
    vt[...] = v_ref[...].T

    def per_query(i, carry):
        at = pl.ds(pl.multiple_of(i * block, block), block)
        q = q_ref[at, :]
        start, place = start_ref[:, at], place_ref[:, at]

        def per_key(j, state):
            top, total, acc = state
            over = pl.ds(pl.multiple_of(j * block, block), block)
            s = dot(k_ref[over, :], q, NT) * scale
            key = j * block + lax.broadcasted_iota(jnp.int32, (block, block), 0)
            s = jnp.where((key >= start) & (key <= place), s, NEG_LARGE)
            new_top = jnp.maximum(top, jnp.max(s, axis=0, keepdims=True))
            p = jnp.exp(s - new_top)
            fade = jnp.exp(top - new_top)
            total = total * fade + jnp.sum(p, axis=0, keepdims=True)
            acc = acc * fade + dot(vt[:, over], p)
            return new_top, total, acc

        begin = (
            jnp.full((1, block), -1e29, F32),
            jnp.zeros((1, block), F32),
            jnp.zeros((HD, block), F32),
        )
        top, total, acc = lax.fori_loop(low_ref[i], high_ref[i] + 1, per_key, begin)
        o_ref[at, :] = (acc / total).T.astype(BF16)
        lse_ref[:, at] = top + jnp.log(total)
        return carry

    lax.fori_loop(0, q_ref.shape[0] // block, per_query, 0)


def attend(q, k, v, low, high, start, place, block):
    smem, vmem = pl.BlockSpec(memory_space=pltpu.SMEM), pl.BlockSpec(memory_space=pltpu.VMEM)
    return pl.pallas_call(
        functools.partial(attend_kernel, block),
        out_shape=[
            jax.ShapeDtypeStruct(q.shape, BF16),
            jax.ShapeDtypeStruct((1, q.shape[0]), F32),
        ],
        in_specs=[smem, smem, vmem, vmem, vmem, vmem, vmem],
        out_specs=[vmem, vmem],
        scratch_shapes=[pltpu.VMEM((HD, k.shape[0]), BF16)],
        compiler_params=pltpu.CompilerParams(vmem_limit_bytes=VMEM_LIMIT),
    )(low, high, q, k, v, start, place)


def attend_back_kernel(
    block, low_ref, high_ref, q_ref, k_ref, v_ref, o_ref, do_ref, lse_ref, start_ref, place_ref,
    dq_ref, dk_ref, dv_ref, kt, dk_acc, dv_acc,
):
    scale = HD**-0.5
    kt[...] = k_ref[...].T
    dk_acc[...] = jnp.zeros_like(dk_acc)
    dv_acc[...] = jnp.zeros_like(dv_acc)

    def per_query(i, carry):
        at = pl.ds(pl.multiple_of(i * block, block), block)
        q, do = q_ref[at, :], do_ref[at, :]
        start, place, lse = start_ref[:, at], place_ref[:, at], lse_ref[:, at]
        delta = jnp.sum((do.astype(F32) * o_ref[at, :].astype(F32)).T, axis=0, keepdims=True)

        def per_key(j, acc):
            over = pl.ds(pl.multiple_of(j * block, block), block)
            k = k_ref[over, :]
            s = dot(k, q, NT) * scale
            key = j * block + lax.broadcasted_iota(jnp.int32, (block, block), 0)
            p = jnp.exp(jnp.where((key >= start) & (key <= place), s - lse, NEG_LARGE))
            dp = dot(v_ref[over, :], do, NT)
            ds = (p * (dp - delta)).astype(BF16)
            dv_acc[over, :] += dot(p, do)
            dk_acc[over, :] += dot(ds, q)
            return acc + dot(kt[:, over], ds)

        acc = lax.fori_loop(low_ref[i], high_ref[i] + 1, per_key, jnp.zeros((HD, block), F32))
        dq_ref[at, :] = (acc * scale).T.astype(BF16)
        return carry

    lax.fori_loop(0, q_ref.shape[0] // block, per_query, 0)
    dk_ref[...] = (dk_acc[...] * scale).astype(BF16)
    dv_ref[...] = dv_acc[...].astype(BF16)


def attend_back(q, k, v, o, do, lse, low, high, start, place, block):
    smem, vmem = pl.BlockSpec(memory_space=pltpu.SMEM), pl.BlockSpec(memory_space=pltpu.VMEM)
    return pl.pallas_call(
        functools.partial(attend_back_kernel, block),
        out_shape=[jax.ShapeDtypeStruct(a.shape, BF16) for a in (q, k, v)],
        in_specs=[smem, smem] + [vmem] * 8,
        out_specs=[vmem] * 3,
        scratch_shapes=[
            pltpu.VMEM((HD, k.shape[0]), BF16),
            pltpu.VMEM(k.shape, F32),
            pltpu.VMEM(v.shape, F32),
        ],
        compiler_params=pltpu.CompilerParams(vmem_limit_bytes=VMEM_LIMIT),
    )(low, high, q, k, v, o, do, lse, start, place)


def rope_tables(positions):
    half = HD // 2
    frequency = ROPE_BASE ** (jnp.arange(half, dtype=F32) * (-2.0 / HD))
    angles = positions.astype(F32)[..., None] * frequency
    return jnp.cos(angles)[:, :, None, :], jnp.sin(angles)[:, :, None, :]


def rotate(values, cosine, sine):
    first, second = values[..., : HD // 2], values[..., HD // 2 :]
    return jnp.concatenate([first * cosine - second * sine, second * cosine + first * sine], axis=-1)


def column_stats(w, a, b):
    aw = dot(a, w, TN)
    bf = b.astype(F32)
    ab = dot(dot(a, a, TN), b)
    wf = w.astype(F32)
    squares = jnp.sum(wf * wf, axis=0) + 2.0 * ADAPT_SCALE * jnp.sum(bf * aw, axis=0)
    squares = squares + ADAPT_SCALE * ADAPT_SCALE * jnp.sum(bf * ab, axis=0)
    return squares, aw + ADAPT_SCALE * ab


def back(e, pre, scale, magnitude, norm, h, low, w, a, b, at_v):
    sums = jnp.sum(e * pre, axis=0)
    dpre = (e * scale).astype(BF16)
    turn = magnitude * sums / (norm * norm * norm)
    tb = (turn[None, :] * b.astype(F32)).astype(BF16)
    dlow = (ADAPT_SCALE * dot(dpre, b, NT)).astype(BF16)
    dh = dot(dpre, w, NT) + dot(dlow, a, NT)
    grad_b = ADAPT_SCALE * (dot(low, dpre, TN) - at_v * turn[None, :])
    v_tb = dot(tb, w, NT) + ADAPT_SCALE * dot(dot(tb, b, NT), a, NT)
    grad_a = dot(dlow, h, TN) - ADAPT_SCALE * v_tb
    return dh, grad_a, grad_b, sums / norm


def per_device(
    tokens, attn_gain, base_qkv, adapt_a_qkv, adapt_b_qkv, magnitude_qkv, base_out, adapt_a_out,
    adapt_b_out, magnitude_out, ffn_gain, base_gu, adapt_a_gu, adapt_b_gu, magnitude_gu, base_down,
    adapt_a_down, adapt_b_down, magnitude_down, doc_lengths, cotangent,
):
    rows_n, group, width = tokens.shape
    count = rows_n * group
    local = base_qkv.shape[2]
    heads = local // HD
    pairs = rows_n * heads
    seq_n = lax.axis_size("seq")
    fan = seq_n // pairs
    length = group * seq_n
    me = lax.axis_index("seq")

    order = jnp.arange(doc_lengths.shape[1])
    doc_ends = jnp.sum(
        jnp.where(order[None, :, None] <= order[None, None, :], doc_lengths[:, :, None], 0), axis=1
    )
    doc_starts = doc_ends - doc_lengths

    def starts_of(places, ends, starts):
        inside = (places[..., None] >= starts) & (places[..., None] < ends)
        return jnp.sum(jnp.where(inside, starts, 0), axis=-1)

    mine = me * group + jnp.arange(group, dtype=jnp.int32)
    position = mine[None, :] - starts_of(
        jnp.broadcast_to(mine[None, :], (rows_n, group)), doc_ends[:, None], doc_starts[:, None]
    )
    cosine, sine = rope_tables(position)
    pair = me // fan
    row = pair // heads
    block_at = lax.rem(me, fan) + fan * jnp.arange(seq_n // fan, dtype=jnp.int32)
    place = (block_at[:, None] * group + jnp.arange(group, dtype=jnp.int32)[None, :]).reshape(-1)
    pick = (jnp.arange(rows_n) == row)[:, None]
    row_ends = jnp.sum(jnp.where(pick, doc_ends, 0), axis=0)
    row_starts = jnp.sum(jnp.where(pick, doc_starts, 0), axis=0)
    start = starts_of(place, row_ends, row_starts)
    low_block = start.reshape(-1, group)[:, 0] // group
    place, start = place[None, :], start[None, :]

    qkv_stats = [column_stats(base_qkv[i], adapt_a_qkv[i], adapt_b_qkv[i]) for i in range(3)]
    gu_stats = [column_stats(base_gu[i], adapt_a_gu[i], adapt_b_gu[i]) for i in range(2)]
    out_squares, out_at_v = column_stats(base_out, adapt_a_out, adapt_b_out)
    down_squares, down_at_v = column_stats(base_down, adapt_a_down, adapt_b_down)
    out_squares, down_squares = lax.psum((out_squares, down_squares), "heads")
    qkv_norm = [jnp.sqrt(s + COLUMN_EPS) for s, _ in qkv_stats]
    gu_norm = [jnp.sqrt(s + COLUMN_EPS) for s, _ in gu_stats]
    out_norm, down_norm = jnp.sqrt(out_squares + COLUMN_EPS), jnp.sqrt(down_squares + COLUMN_EPS)
    qkv_scale = [magnitude_qkv[i] / qkv_norm[i] for i in range(3)]
    gu_scale = [magnitude_gu[i] / gu_norm[i] for i in range(2)]
    out_scale, down_scale = magnitude_out / out_norm, magnitude_down / down_norm

    x = tokens.astype(F32).reshape(count, width)
    inverse_one = lax.rsqrt(jnp.mean(x * x, axis=-1, keepdims=True) + NORM_EPS)
    h1 = (x * inverse_one * attn_gain).astype(BF16)
    qkv_low = [dot(h1, adapt_a_qkv[i]).astype(BF16) for i in range(3)]
    qkv_pre = [
        dot(h1, base_qkv[i]) + ADAPT_SCALE * dot(qkv_low[i], adapt_b_qkv[i]) for i in range(3)
    ]
    shaped = [
        (qkv_pre[i] * qkv_scale[i]).reshape(rows_n, group, heads, HD) for i in range(3)
    ]
    shaped = [rotate(shaped[0], cosine, sine), rotate(shaped[1], cosine, sine), shaped[2]]
    q, k, v = exchange(
        ("queries", "keys", "keys"),
        [s.transpose(0, 2, 1, 3).reshape(pairs, group, HD).astype(BF16) for s in shaped],
        pairs,
        1,
    )
    q, k, v = q.reshape(-1, HD), k.reshape(length, HD), v.reshape(length, HD)
    o, lse = attend(q, k, v, low_block, block_at, start, place, group)
    [attn] = exchange(("queries_back",), [o.reshape(-1, group, HD)], pairs, 2)
    attn = attn.reshape(rows_n, heads, group, HD).transpose(0, 2, 1, 3).reshape(count, local)

    out_low = dot(attn, adapt_a_out).astype(BF16)
    out_pre = line_sum(
        (dot(attn, base_out) + ADAPT_SCALE * dot(out_low, adapt_b_out)).astype(BF16), 3
    ).astype(F32)
    x2 = x + out_pre * out_scale
    inverse_two = lax.rsqrt(jnp.mean(x2 * x2, axis=-1, keepdims=True) + NORM_EPS)
    h2 = (x2 * inverse_two * ffn_gain).astype(BF16)

    gu_low = [dot(h2, adapt_a_gu[i]).astype(BF16) for i in range(2)]
    gu_pre = [dot(h2, base_gu[i]) + ADAPT_SCALE * dot(gu_low[i], adapt_b_gu[i]) for i in range(2)]
    gate, up = gu_pre[0] * gu_scale[0], gu_pre[1] * gu_scale[1]
    sigma = jax.nn.sigmoid(gate)
    z = (gate * sigma * up).astype(BF16)
    down_low = dot(z, adapt_a_down).astype(BF16)
    down_part = (dot(z, base_down) + ADAPT_SCALE * dot(down_low, adapt_b_down)).astype(BF16)
    dy = cotangent.astype(F32).reshape(count, width)
    down_dpre = (dy * down_scale).astype(BF16)
    down_dlow = (ADAPT_SCALE * dot(down_dpre, adapt_b_down, NT)).astype(BF16)
    dz = dot(down_dpre, base_down, NT) + dot(down_dlow, adapt_a_down, NT)
    dgate = dz * up * sigma * (1.0 + gate * (1.0 - sigma))
    dup = dz * gate * sigma
    gu_back = [
        back(
            e, gu_pre[i], gu_scale[i], magnitude_gu[i], gu_norm[i], h2, gu_low[i], base_gu[i],
            adapt_a_gu[i], adapt_b_gu[i], gu_stats[i][1],
        )
        for i, e in enumerate((dgate, dup))
    ]
    dh2 = line_sum((gu_back[0][0] + gu_back[1][0]).astype(BF16), 4).astype(F32)
    down_pre = lax.psum(down_part, "heads").astype(F32)
    mixed = (x2 + down_pre * down_scale).astype(BF16)
    down_sums = jnp.sum(dy * down_pre, axis=0)
    down_turn = magnitude_down * down_sums / (down_norm * down_norm * down_norm)
    down_tb = (down_turn[None, :] * adapt_b_down.astype(F32)).astype(BF16)
    down_v_tb = dot(down_tb, base_down, NT) + ADAPT_SCALE * dot(
        dot(down_tb, adapt_b_down, NT), adapt_a_down, NT
    )
    grad_a_down = dot(down_dlow, z, TN) - ADAPT_SCALE * down_v_tb
    grad_b_down = ADAPT_SCALE * (dot(down_low, down_dpre, TN) - down_at_v * down_turn[None, :])

    scaled = dh2 * ffn_gain
    dx2 = dy + inverse_two * scaled - x2 * inverse_two**3 * jnp.mean(scaled * x2, axis=-1, keepdims=True)
    grad_ffn_gain = jnp.sum(dh2 * x2 * inverse_two, axis=0)

    dattn, grad_a_out, grad_b_out, grad_m_out = back(
        dx2, out_pre, out_scale, magnitude_out, out_norm, attn, out_low, base_out, adapt_a_out,
        adapt_b_out, out_at_v,
    )
    dattn = dattn.astype(BF16).reshape(rows_n, group, heads, HD).transpose(0, 2, 1, 3)
    [do] = exchange(("queries",), [dattn.reshape(pairs, group, HD)], pairs, 5)
    dq, dk, dv = attend_back(
        q, k, v, o, do.reshape(-1, HD), lse, low_block, block_at, start, place, group
    )
    dq, dk, dv = exchange(
        ("queries_back", "keys_back", "keys_back"),
        [dq.reshape(-1, group, HD), dk.reshape(-1, group, HD), dv.reshape(-1, group, HD)],
        pairs,
        6,
    )
    dk, dv = [jnp.sum(a.reshape(pairs, fan, group, HD).astype(F32), axis=1) for a in (dk, dv)]
    dq, dk, dv = [
        a.astype(F32).reshape(rows_n, heads, group, HD).transpose(0, 2, 1, 3) for a in (dq, dk, dv)
    ]
    grads = [
        a.reshape(count, local) for a in (rotate(dq, cosine, -sine), rotate(dk, cosine, -sine), dv)
    ]
    qkv_back = [
        back(
            grads[i], qkv_pre[i], qkv_scale[i], magnitude_qkv[i], qkv_norm[i], h1, qkv_low[i],
            base_qkv[i], adapt_a_qkv[i], adapt_b_qkv[i], qkv_stats[i][1],
        )
        for i in range(3)
    ]
    dh1 = line_sum((qkv_back[0][0] + qkv_back[1][0] + qkv_back[2][0]).astype(BF16), 7).astype(F32)
    scaled = dh1 * attn_gain
    dx = dx2 + inverse_one * scaled - x * inverse_one**3 * jnp.mean(scaled * x, axis=-1, keepdims=True)
    grad_attn_gain = jnp.sum(dh1 * x * inverse_one, axis=0)

    both = [
        jnp.stack([qkv_back[i][1] for i in range(3)]),
        jnp.stack([gu_back[i][1] for i in range(2)]),
        grad_b_out,
        grad_b_down,
    ]
    both = lax.psum([a.astype(BF16) for a in both], ("seq", "heads"))
    over_seq = [
        jnp.stack([qkv_back[i][2] for i in range(3)]),
        jnp.stack([qkv_back[i][3] for i in range(3)]),
        grad_a_out,
        grad_m_out,
        jnp.stack([gu_back[i][2] for i in range(2)]),
        jnp.stack([gu_back[i][3] for i in range(2)]),
        grad_a_down,
        down_sums / down_norm,
        grad_ffn_gain,
        grad_attn_gain,
    ]
    over_seq = lax.psum([a.astype(BF16) for a in over_seq], "seq")
    both = [a.astype(F32) for a in both]
    over_seq = [a.astype(F32) for a in over_seq]
    return (
        mixed.reshape(rows_n, group, width),
        dx.reshape(rows_n, group, width),
        over_seq[9],
        both[0].transpose(0, 2, 1),
        over_seq[0],
        over_seq[1],
        over_seq[2].T,
        both[2],
        over_seq[3],
        over_seq[8],
        both[1].transpose(0, 2, 1),
        over_seq[4],
        over_seq[5],
        over_seq[6].T,
        both[3],
        over_seq[7],
    )


def solution(mesh):
    in_specs = (
        P(None, "seq", None), P(), P(None, None, "heads"), P(), P(None, None, "heads"), P(None, "heads"),
        P("heads", None), P("heads", None), P(), P(), P(), P(None, None, "heads"), P(),
        P(None, None, "heads"), P(None, "heads"), P("heads", None), P("heads", None), P(), P(), P(),
        P(None, "seq", None),
    )
    out_specs = (
        P(None, "seq", None), P(None, "seq", None), P(), P(), P(None, None, "heads"), P(None, "heads"),
        P("heads", None), P(), P(), P(), P(), P(None, None, "heads"), P(None, "heads"),
        P("heads", None), P(), P(),
    )
    return jax.shard_map(
        per_device, mesh=mesh, in_specs=in_specs, out_specs=out_specs, check_vma=False
    )
```

time: 996 us -> 849 us (0.85)
  Pallas kernels: 0 us -> 385 us
  waiting for transfers between devices: 536 us -> 172 us
  matrix products: 236 us -> 139 us
  blocking collectives: 59.8 us -> 20.8 us
  local copies, waits for them, and re-layouts: 61.8 us -> 24.4 us
  other arithmetic: 57.7 us -> 83.7 us
  loops' own time: 17.3 us -> 0 us
    pallas_call x0 -> x9, Pallas kernels: none -> 385 us  [the longest x3 280 us: line_sum(): pl.pallas_call(functools.partial(line_sum_kernel, depth, chunks, rows), o...]
    psum x6 -> x4, waiting for transfers between devices: 414 us -> 171 us  [the longest x1 123 us: per_device(): both = lax.psum([a.astype(BF16) for a in both], ('seq', 'heads'))]
    dot_general x81 -> x84, matrix products: 236 us -> 139 us  [dot(): lax.dot_general(a.astype(BF16), b.astype(BF16), dims, preferred_element_t...]
    reduce_scatter x1 -> x0, waiting for transfers between devices: 89 us -> none  [per_device(): lax.psum_scatter(terms.astype(jnp.bfloat16), 'seq', scatter_dimension=1,...]
    psum x3 -> x1, blocking collectives: 59.8 us -> 20.8 us  [per_device(): out_squares, down_squares = lax.psum((out_squares, down_squares), 'heads')]
    all_gather x2 -> x0, waiting for transfers between devices: 33 us -> none  [the longest x1 24 us: per_device(): lax.all_gather(value_b, 'seq', axis=1, tiled=True)]
    another operation x15 -> x0, loops' own time: 17.3 us -> none  [the longest x1 5.64 us: per_device(): lax.scan(back_step, start_state, jnp.arange(block_count, dtype=jnp.int32))]
    reduce_sum x22 -> x16, other arithmetic: 12.3 us -> 29.5 us  [the longest x4 12 us: column_stats(): jnp.sum(wf * wf, axis=0) + 2.0 * ADAPT_SCALE * jnp.sum(bf * aw, axis=0)]
  transfers between devices with their start and end apart: 9 -> 4, of which waited for: 9 -> 2; matrix products, arithmetic and copies ran while one was open for 12% -> 8% of each run, Pallas kernels for 0% -> 15%
where the time goes in v1:
time: 849 us; the launch traced here: 841 us
  Pallas kernels  385 us (45%)
  waiting for transfers between devices  172 us (20%)
  matrix products  139 us (16%)
  other arithmetic  83.7 us (10%)
  local copies, waits for them, and re-layouts  24.4 us (3%)
  blocking collectives  20.8 us (2%)
  between operations  15.8 us (2%)
    pallas_call x3, Pallas kernels, line_sum(): pl.pallas_call(functools.partial(line_sum_kernel, depth, chunks, rows), o...  280 us
    dot_general x84, matrix products, dot(): lax.dot_general(a.astype(BF16), b.astype(BF16), dims, preferred_element_t...  139 us
    psum x1, waiting for transfers between devices, per_device(): both = lax.psum([a.astype(BF16) for a in both], ('seq', 'heads'))  123 us
    pallas_call x4, Pallas kernels, exchange(): pl.pallas_call(functools.partial(exchange_kernel, kinds, seq_n, pairs), o...  69.6 us
    psum x2, waiting for transfers between devices, per_device(): over_seq = lax.psum([a.astype(BF16) for a in over_seq], 'seq')  48.6 us
    psum x1, blocking collectives, per_device(): out_squares, down_squares = lax.psum((out_squares, down_squares), 'heads')  20.8 us
    pallas_call x1, Pallas kernels, attend_back(): pl.pallas_call(functools.partial(attend_back_kernel, block), out_shape=[j...  18.6 us
  transfers between devices with their start and end apart: 4, of which 2 were waited for; matrix products, arithmetic and copies ran while one was open for 8% of the time, Pallas kernels for 15%

profile of v1, /device:TPU:0, one launch (start us, length us, event | category | flops | bytes accessed | tf_op | source)
XLA Modules:
  0.0 840.5 jit_solution(1347123664400452842)
XLA Ops:
  7.8 3.6 multiply_reduce_fusion.5
  14.9 6.7 multiply_reduce_fusion.2
  22.6 1.5 fusion.4
  30.9 3.9 fusion.92
  34.7 2.2 fusion.100
  37.0 2.2 fusion.108
  41.8 4.2 fusion.190
  46.3 2.7 fusion.187
  49.0 20.8 %all-reduce = (f32[2048]{0:T(1024)S(1)}, f32[2048]{0:T(1024)S(1)}) all-reduce(f32[2048]{0:T(1024)S(1)} %multiply_add_fusion.3, f32[2048]{0:T(1024)S(1)} %multiply_add_fusion.2), channel_id=1, replica_groups=mesh['seq'=8,'heads'=4] {'heads'}, use_global_device_ids=true, to_apply=%region_18.19 | all-reduce | flops 4096 | bytes 32768 | tf_op jit(solution)/shard_map/psum | solution.py:408
  69.9 2.0 fusion.32
  73.3 7.7 fusion.382
  83.3 2.6 fusion.297
  90.0 2.9 broadcast_multiply_fusion.1
  93.0 1.6 reshape.933
  94.5 2.9 broadcast_multiply_fusion
  97.5 2.6 reshape.934
  100.0 2.4 fusion.205
  102.4 3.4 subtract_convert_fusion
  109.1 23.1 %shard_map.324 = (bf16[8,256,128]{2,1,0:T(8,128)(2,1)}, bf16[8,256,128]{2,1,0:T(8,128)(2,1)}, bf16[8,256,128]{2,1,0:T(8,128)(2,1)}) custom-call(bf16[8,256,128]{2,1,0:T(8,128)(2,1)} %bitcast.531, bf16[8,256,128]{2,1,0:T(8,128)(2,1)} %bitcast.530, bf16[8,256,128]{2,1,0:T(8,128)(2,1)} %bitcast.528), custom_call_target="tpu_custom_call" | custom-call | tf_op jit(solution)/shard_map/pallas_call | solution.py:95
  132.7 16.5 %shard_map.325 = (bf16[2048,128]{1,0:T(8,128)(2,1)}, f32[1,2048]{1,0:T(1,128)}) custom-call(s32[8]{0:T(128)} %and_select_fusion.low_ref, s32[8]{0:T(128)} %iota.53.high_ref, bf16[2048,128]{1,0:T(8,128)(2,1)} %bitcast.532, bf16[2048,128]{1,0:T(8,128)(2,1)} %bitcast.534, bf16[2048,128]{1,0:T(8,128)(2,1)} %bitcast.536, s32[1,2048]{1,0:T(1,128)} %bitcast.545, ...), custom_call_target="tpu_custom_call" | custom-call | tf_op jit(solution)/shard_map/pallas_call | solution.py:263
  149.2 11.0 %shard_map.326 = bf16[8,256,128]{2,1,0:T(8,128)(2,1)} custom-call(bf16[8,256,128]{2,1,0:T(8,128)(2,1)} %bitcast.527), custom_call_target="tpu_custom_call" | custom-call | tf_op jit(solution)/shard_map/pallas_call | solution.py:95
  160.2 1.4 copy.65
  163.2 2.0 add_convert_fusion.3.x_ref
  165.2 78.0 %shard_map.327 = bf16[512,2048]{1,0:T(8,128)(2,1)} custom-call(bf16[512,2048]{1,0:T(8,128)(2,1)} %add_convert_fusion.3.x_ref), custom_call_target="tpu_custom_call" | custom-call | tf_op jit(solution)/shard_map/pallas_call | solution.py:207
  243.2 2.7 multiply_reduce_fusion.3
  249.1 6.2 fusion.6
  255.3 3.4 fusion.14
  261.3 3.7 multiply_reduce_fusion.9
  267.9 1.8 convolution_convert_fusion
  269.7 5.9 fusion.381
  275.6 2.0 add_convert_fusion.2
  277.7 1.8 fusion.121
  279.6 4.3 fusion.8
  283.8 4.4 fusion
  288.7 7.9 fusion.10
  296.6 5.0 fusion.2
  303.0 1.5 copy-done.28
  304.5 4.5 add_convert_fusion.1.x_ref
  309.0 124.2 %shard_map.328 = bf16[512,2048]{1,0:T(8,128)(2,1)} custom-call(bf16[512,2048]{1,0:T(8,128)(2,1)} %add_convert_fusion.1.x_ref), custom_call_target="tpu_custom_call" | custom-call | tf_op jit(solution)/shard_map/pallas_call | solution.py:207
  435.5 2.4 fusion.29
  439.5 1.6 convert_element_type.505
  441.1 6.7 fusion.25
  448.3 1.6 copy-done.8
  454.3 12.1 %shard_map.329 = bf16[8,256,128]{2,1,0:T(8,128)(2,1)} custom-call(bf16[8,256,128]{2,1,0:T(8,128)(2,1)} %bitcast.538), custom_call_target="tpu_custom_call" | custom-call | tf_op jit(solution)/shard_map/pallas_call | solution.py:95
  467.0 18.6 %shard_map.330 = (bf16[2048,128]{1,0:T(8,128)(2,1)}, bf16[2048,128]{1,0:T(8,128)(2,1)}, bf16[2048,128]{1,0:T(8,128)(2,1)}) custom-call(s32[8]{0:T(128)} %and_select_fusion.low_ref, s32[8]{0:T(128)} %iota.56.high_ref, bf16[2048,128]{1,0:T(8,128)(2,1)} %bitcast.533, bf16[2048,128]{1,0:T(8,128)(2,1)} %bitcast.535, bf16[2048,128]{1,0:T(8,128)(2,1)} %bitcast.537, ...), custom_call_target="tpu_custom_call" | custom-call | tf_op jit(solution)/shard_map/pallas_call | solution.py:314
  485.6 23.4 %shard_map.331 = (bf16[8,256,128]{2,1,0:T(8,128)(2,1)}, bf16[8,256,128]{2,1,0:T(8,128)(2,1)}, bf16[8,256,128]{2,1,0:T(8,128)(2,1)}) custom-call(bf16[8,256,128]{2,1,0:T(8,128)(2,1)} %bitcast.540, bf16[8,256,128]{2,1,0:T(8,128)(2,1)} %bitcast.541, bf16[8,256,128]{2,1,0:T(8,128)(2,1)} %bitcast.542), custom_call_target="tpu_custom_call" | custom-call | tf_op jit(solution)/shard_map/pallas_call | solution.py:95
  509.1 1.6 copy.69
  513.0 1.6 multiply_subtract_fusion.1
  521.8 3.3 fusion.96
  526.0 3.4 fusion.104
  530.9 3.3 fusion.88
  535.5 1.6 fusion.195
  544.4 1.5 copy-done.13
  545.9 4.8 add_convert_fusion.x_ref
  550.6 77.7 %shard_map.332 = bf16[512,2048]{1,0:T(8,128)(2,1)} custom-call(bf16[512,2048]{1,0:T(8,128)(2,1)} %add_convert_fusion.x_ref), custom_call_target="tpu_custom_call" | custom-call | tf_op jit(solution)/shard_map/pallas_call | solution.py:207
  628.4 3.9 fusion.31
  638.0 6.1 fusion.21
  644.0 48.6 %all-reduce.14.cloned.1.call-done = (bf16[2048]{0:T(1024)(128)(2,1)}, bf16[3,16,512]{2,1,0:T(8,128)(2,1)}, bf16[3,512]{1,0:T(4,128)(2,1)}, bf16[512,16]{0,1:T(8,...) async-done(((bf16[2048]{0:T(1024)(128)(2,1)}, ...) | async-done | bytes 135696 | tf_op jit(solution)/shard_map/psum | solution.py:535
  703.1 1.4 convert_element_type.486
  704.5 122.6 %all-reduce.12.cloned.1.call-done = (bf16[3,2048,16]{1,2,0:T(8,128)(2,1)}, bf16[16,2048]{1,0:T(8,128)(2,1)}, bf16[2,2048,16]{1,2,0:T(8,128)(2,1)}, bf16[16,2048]{1,0:T(8,128)(2,1)}) async-done(((bf16[3,2048,16]{1,2,0:T(8,128)(2,1)}, bf16[16,2048]{1,0:T(8,128)(2,1)}, bf16[2,2048,16]{1,2,0:T(8,128)(2,1)}, bf16[16,2048]{1,0:T(8,128)(2,1)}), (bf16[3,2048,16]{1,2,0:T(8,128)(2,1)}, bf16[16,2048]{1,0:T(8,128)(2,1)}, ...) | async-done | bytes 458768 | tf_op jit(solution)/shard_map/psum | solution.py:522
  827.2 1.5 convert_element_type.492
  828.7 1.5 convert_element_type.511
  830.2 1.7 transpose.111
  831.9 1.6 transpose.115
  (429 shorter events, 83.2 us)
Async XLA Ops:
  7.2 33.7 %copy-start = (bf16[1408,16]{0,1:T(8,128)(2,1)S(1)}, bf16[1408,16]{0,1:T(8,128)(2,1)}, u32[]{:S(2)}) copy-start(bf16[1408,16]{0,1:T(8,128)(2,1)} %param.37) | copy-start | bytes 135172
  7.2 432.3 %all-reduce.10.cloned.1.call-start = ((), (), s32[]{:S(2)}) async-start(), calls=%async_computation.1 | async-start | bytes 180224 | tf_op jit(solution)/shard_map/psum | solution.py:535
  7.8 4.7 copy-start.3
  7.8 5.9 copy-start.33
  13.7 69.6 %copy-start.56 = (f32[16,512]{1,0:T(8,128)}, f32[16,512]{1,0:T(8,128)S(1)}, u32[]{:S(2)}) copy-start(f32[16,512]{1,0:T(8,128)S(1)} %fusion.106) | copy-start | bytes 98308
  14.1 69.2 %copy-start.58 = (f32[16,512]{1,0:T(8,128)}, f32[16,512]{1,0:T(8,128)S(1)}, u32[]{:S(2)}) copy-start(f32[16,512]{1,0:T(8,128)S(1)} %fusion.98) | copy-start | bytes 98308
  14.3 69.0 %copy-start.69 = (f32[16,512]{1,0:T(8,128)}, f32[16,512]{1,0:T(8,128)S(1)}, u32[]{:S(2)}) copy-start(f32[16,512]{1,0:T(8,128)S(1)} %fusion.135) | copy-start | bytes 98308
  14.3 7.4 copy-start.29
  14.6 68.7 %copy-start.71 = (f32[16,512]{1,0:T(8,128)}, f32[16,512]{1,0:T(8,128)S(1)}, u32[]{:S(2)}) copy-start(f32[16,512]{1,0:T(8,128)S(1)} %fusion.136) | copy-start | bytes 98308
  14.9 68.4 %copy-start.67 = (f32[16,512]{1,0:T(8,128)}, f32[16,512]{1,0:T(8,128)S(1)}, u32[]{:S(2)}) copy-start(f32[16,512]{1,0:T(8,128)S(1)} %fusion.137) | copy-start | bytes 98308
  14.9 7.8 copy-start.2
  22.6 3.4 copy-start.1
  22.6 4.5 copy-start.82
  27.1 7.6 slice-start.6
  28.3 59.4 %copy-start.60 = (bf16[512,16]{0,1:T(8,128)(2,1)}, bf16[512,16]{0,1:T(8,128)(2,1)S(1)}, u32[]{:S(2)}) copy-start(bf16[512,16]{0,1:T(8,128)(2,1)S(1)} %convolution_convert_fusion.3) | copy-start | bytes 49156
  29.6 5.1 slice-start.7
  34.7 4.9 slice-start.10
  41.8 4.2 copy-start.32
  41.8 4.2 copy-start.53
  41.8 28.0 %copy-start.95 = (f32[2048]{0:T(1024)S(1)}, f32[2048]{0:T(1024)}, u32[]{:S(2)}) copy-start(f32[2048]{0:T(1024)} %param.30) | copy-start | bytes 24580
  41.8 28.0 %copy-start.97 = (f32[2048]{0:T(1024)S(1)}, f32[2048]{0:T(1024)}, u32[]{:S(2)}) copy-start(f32[2048]{0:T(1024)} %param.39) | copy-start | bytes 24580
  46.3 25.6 %copy-start.38 = (f32[16,2048]{1,0:T(8,128)}, f32[16,2048]{1,0:T(8,128)S(1)}, u32[]{:S(2)}) copy-start(f32[16,2048]{1,0:T(8,128)S(1)} %fusion.138) | copy-start | bytes 393220
  69.8 3.4 copy-start.99
  69.8 3.4 copy-start.101
  69.9 3.4 copy-start.80
  73.2 7.7 copy-start.128
  73.2 13.9 %copy-start.117 = (f32[3,512]{1,0:T(4,128)S(1)}, f32[3,512]{1,0:T(4,128)}, u32[]{:S(2)}) copy-start(f32[3,512]{1,0:T(4,128)} %param.26) | copy-start | bytes 18436
  82.6 6.5 copy-start.74
  82.6 5.1 copy-start.42
  102.4 3.4 copy-start.36
  109.0 52.6 %copy-start.54 = (bf16[512,16]{0,1:T(8,128)(2,1)S(1)}, bf16[512,16]{0,1:T(8,128)(2,1)}, u32[]{:S(2)}) copy-start(bf16[512,16]{0,1:T(8,128)(2,1)} %param.28) | copy-start | bytes 49156
  109.0 52.8 %copy-start.10 = (bf16[512,2048]{1,0:T(8,128)(2,1)S(1)}, bf16[512,2048]{1,0:T(8,128)(2,1)}, u32[]{:S(2)}) copy-start(bf16[512,2048]{1,0:T(8,128)(2,1)} %param.27) | copy-start | bytes 6291460
  247.8 7.5 copy-start.6
  248.4 6.9 slice-start
  249.1 6.2 slice-start.1
  249.1 6.2 slice-start.2
  255.3 3.4 copy-start.35
  255.3 3.4 copy-start.64
  266.1 9.5 %copy-start.75 = (f32[1408]{0:T(1024)}, f32[1408]{0:T(1024)S(1)}, u32[]{:S(2)}) copy-start(f32[1408]{0:T(1024)S(1)} %get-tuple-element.63) | copy-start | bytes 16900
  267.6 173.4 %all-reduce.8.cloned.1.call-start = ((), (), s32[]{:S(2)}) async-start(), calls=%async_computation | async-start | bytes 4194304 | tf_op jit(solution)/shard_map/psum | solution.py:467
  269.7 5.9 copy-start.65
  277.7 415.0 %all-reduce.14.cloned.1.call-start = ((), (), s32[]{:S(2)}) async-start(), calls=%async_computation.3 | async-start | bytes 273408 | tf_op jit(solution)/shard_map/psum | solution.py:535
  283.8 4.4 copy-start.21
  283.8 12.8 %slice-start.3 = ((s8[11534336]{0:T(1024)(128)(4,1)}), s8[4194304]{0:T(1024)(128)(4,1)S(1)}, s32[]{:S(2)}) async-start(s8[11534336]{0:T(1024)(128)(4,1)} %bitcast.490), calls=%async_computation.7 | async-start | bytes 8388608
  288.7 7.9 slice-start.4
  288.7 7.9 slice-start.5
  288.7 7.9 copy-start.24
  296.6 5.0 copy-start.126
  301.6 132.4 %copy-start.107 = (f32[1,2,2,128]{3,1,2,0:T(2,128)}, f32[1,2,2,128]{3,1,2,0:T(2,128)S(1)}, u32[]{:S(2)}) copy-start(f32[1,2,2,128]{3,1,2,0:T(2,128)S(1)} %copy.73) | copy-start | bytes 6148
  309.0 124.2 %copy-start.7 = (bf16[512,2048]{1,0:T(8,128)(2,1)S(1)}, bf16[512,2048]{1,0:T(8,128)(2,1)}, u32[]{:S(2)}) copy-start(bf16[512,2048]{1,0:T(8,128)(2,1)} %copy-done.6) | copy-start | bytes 6291460
  435.5 3.7 copy-start.22
  435.5 5.6 copy-start.81
  435.5 5.6 copy-start.119
  509.1 3.6 copy-start.25
  513.0 5.8 slice-start.8
  514.6 4.2 slice-start.9
  526.0 9.5 %slice-start.12 = ((s8[5767168]{0:T(1024)(128)(4,1)}), s8[4194304]{0:T(1024)(128)(4,1)S(1)}, s32[]{:S(2)}) async-start(s8[5767168]{0:T(1024)(128)(4,1)} %bitcast.498), calls=%async_computation.16 | async-start | bytes 8388608
  529.3 6.1 slice-start.13
  530.9 3.9 copy-start.98
  530.9 3.9 copy-start.100
  550.6 77.7 %copy-start.83 = (f32[2048]{0:T(1024)S(1)}, f32[2048]{0:T(1024)}, u32[]{:S(2)}) copy-start(f32[2048]{0:T(1024)} %param.22) | copy-start | bytes 24580
  550.6 77.7 %copy-start.108 = (f32[1,2,2,128]{3,1,2,0:T(2,128)S(1)}, f32[1,2,2,128]{3,1,2,0:T(2,128)}, u32[]{:S(2)}) copy-start(f32[1,2,2,128]{3,1,2,0:T(2,128)} %copy-done.107) | copy-start | bytes 6148
  632.8 5.2 copy-start.127
  637.4 189.8 %all-reduce.12.cloned.1.call-start = ((), (), s32[]{:S(2)}) async-start(), calls=%async_computation.2 | async-start | bytes 917504 | tf_op jit(solution)/shard_map/psum | solution.py:522
  (83 other events, 163.3 us)
Sparse Core Ops, SparseCore 0:
  267.8 51.1 all-reduce.9
  321.5 110.3 all-reduce.7
  637.5 55.1 all-reduce.13
  699.5 127.6 all-reduce.11

commit v2 on v1

v2 whole, which is shorter than its diff:
```python
import functools

import jax
import jax.numpy as jnp
from jax import lax
from jax.experimental import pallas as pl
from jax.experimental.pallas import tpu as pltpu
from jax.sharding import PartitionSpec as P

HD = 128
RANK = 16
ADAPT_SCALE = 2.0
NORM_EPS = 1e-05
COLUMN_EPS = 1e-06
ROPE_BASE = 10000.0
NEG_LARGE = -1e30
F32 = jnp.float32
BF16 = jnp.bfloat16
MESH = pl.DeviceIdType.MESH
NN = (((1,), (0,)), ((), ()))
NT = (((1,), (1,)), ((), ()))
TN = (((0,), (0,)), ((), ()))
OWNERS = 8
IN_VMEM = pl.BlockSpec(memory_space=pltpu.VMEM)
IN_SMEM = pl.BlockSpec(memory_space=pltpu.SMEM)
ANYWHERE = pl.BlockSpec(memory_space=pl.ANY)


def dot(a, b, dims=NN):
    return lax.dot_general(a.astype(BF16), b.astype(BF16), dims, preferred_element_type=F32)


def shape(*dims, dtype=BF16):
    return jax.ShapeDtypeStruct(dims, dtype)


def dma(*dims):
    return pltpu.SemaphoreType.DMA(dims)


def params(mib, collective_id=None):
    more = {} if collective_id is None else {"collective_id": collective_id, "has_side_effects": True}
    return pltpu.CompilerParams(vmem_limit_bytes=mib * 2**20, **more)


def tiles(count, size, body):
    whole = count // size
    if whole:

        def step(t, carry):
            body(pl.ds(pl.multiple_of(t * size, 128), size), t)
            return carry

        lax.fori_loop(0, whole, step, 0)
    if count - whole * size:
        body(pl.ds(whole * size, count - whole * size), whole)


def row_loop(count, size, body, init=0):
    def step(t, carry):
        return body(pl.ds(pl.multiple_of(t * size, size), size), carry)

    return lax.fori_loop(0, count // size, step, init)


def fold(v):
    return jnp.sum(v.reshape(v.shape[0] // 8, 8, v.shape[1]), axis=0)


def total(v):
    return jnp.sum(v, axis=0, keepdims=True)


def greet(seq=0, heads=0, line=0):
    barrier = pltpu.get_barrier_semaphore()
    me, h = lax.axis_index("seq"), lax.axis_index("heads")
    peers = 0
    for d in range(1, seq):
        pl.semaphore_signal(barrier, inc=1, device_id={"seq": lax.rem(me + d, seq)}, device_id_type=MESH)
        peers = peers + 1
    for d in range(1, heads):
        pl.semaphore_signal(
            barrier, inc=1, device_id={"heads": lax.rem(h + d, heads)}, device_id_type=MESH
        )
        peers = peers + 1
    if line:
        for step in (-1, 1):

            @pl.when((h + step >= 0) & (h + step < line))
            def _(step=step):
                pl.semaphore_signal(barrier, inc=1, device_id={"heads": h + step}, device_id_type=MESH)

        peers = peers + jnp.where((h == 0) | (h == line - 1), 1, 2)
    pl.semaphore_wait(barrier, peers)


def remote(src, dst, send_sem, recv_sem, **where):
    return pltpu.make_async_remote_copy(
        src_ref=src, dst_ref=dst, send_sem=send_sem, recv_sem=recv_sem, device_id=where, device_id_type=MESH
    )


class Exchange:
    def __init__(self, kind, seq_n, pairs, src, dst, send_sem, recv_sem):
        fan = seq_n // pairs
        me = lax.axis_index("seq")
        self.me, self.src, self.dst, self.send_sem, self.recv_sem = me, src, dst, send_sem, recv_sem
        self.count = self.slots(kind, seq_n, pairs)
        self.target, self.block, self.slot = {
            "queries": (lambda p: p * fan + lax.rem(me, fan), lambda p: p, me // fan),
            "keys": (lambda e: e, lambda e: e // fan, me),
            "queries_back": (lambda i: lax.rem(me, fan) + fan * i, lambda i: i, me // fan),
            "keys_back": (lambda e: e, lambda e: e, me),
        }[kind]

    @staticmethod
    def slots(kind, seq_n, pairs):
        return pairs if kind.startswith("queries") else seq_n

    def copy(self, j):
        return remote(
            self.src(self.block(j)),
            self.dst(self.slot),
            self.send_sem.at[j],
            self.recv_sem.at[self.slot],
            seq=self.target(j),
        )

    def start(self):
        def one(d, carry):
            j = lax.rem(self.me + d, self.count)

            @pl.when(self.target(j) != self.me)
            def _():
                self.copy(j).start()

            @pl.when(self.target(j) == self.me)
            def _():
                pltpu.make_async_copy(
                    self.src(self.block(j)), self.dst(self.slot), self.recv_sem.at[self.slot]
                ).start()

            return carry

        lax.fori_loop(0, self.count, one, 0)

    def wait_recv(self):
        def one(j, carry):
            pltpu.make_async_copy(self.dst(j), self.dst(j), self.recv_sem.at[j]).wait()
            return carry

        lax.fori_loop(0, self.count, one, 0)

    def wait_send(self):
        def one(j, carry):
            @pl.when(self.target(j) != self.me)
            def _():
                self.copy(j).wait_send()

            return carry

        lax.fori_loop(0, self.count, one, 0)


class Line:
    def __init__(self, depth, x, out, got, held, up_send, up_recv, down_send, down_recv, lag=2):
        self.depth, self.x, self.out, self.got, self.held, self.lag = depth, x, out, got, held, lag
        self.sems = up_send, up_recv, down_send, down_recv
        self.chunks, self.rows = got.shape[1], got.shape[2]
        self.steps = self.chunks + lag * (2 * depth - 3)
        self.h = lax.axis_index("heads")

    @staticmethod
    def scratch(count, width, rows):
        chunks = count // (2 * rows)
        return [pltpu.VMEM((2, chunks, rows, width), BF16)] * 2 + [dma(2, chunks)] * 4

    def ends(self, stream):
        if stream == 0:
            return self.h, self.h + 1, self.h - 1
        return self.depth - 1 - self.h, self.h - 1, self.h + 1

    def place(self, stream, c):
        rows = self.rows
        return pl.ds(pl.multiple_of((1 - stream) * self.chunks * rows + c * rows, rows), rows)

    def up(self, stream, c, src, to):
        return remote(
            src, self.got.at[stream, c], self.sems[0].at[stream, c], self.sems[1].at[stream, c], heads=to
        )

    def down(self, stream, c, to):
        part = self.out.at[self.place(stream, c)]
        return remote(part, part, self.sems[2].at[stream, c], self.sems[3].at[stream, c], heads=to)

    def first(self):
        def one(c, carry):
            for stream in range(2):
                pos, ahead, behind = self.ends(stream)

                @pl.when(pos == 0)
                def _():
                    self.up(stream, c, self.x.at[self.place(stream, c)], ahead).start()

            return carry

        lax.fori_loop(0, self.chunks, one, 0)

    def step(self, t):
        depth, lag = self.depth, self.lag
        for stream in range(2):
            pos, ahead, behind = self.ends(stream)
            c = t - (pos - 1) * lag

            @pl.when((c >= 0) & (c < self.chunks) & (pos > 0))
            def _():
                self.up(stream, c, self.held.at[stream, c], self.h).wait_recv()
                value = self.got[stream, c].astype(F32) + self.x[self.place(stream, c), :].astype(F32)

                @pl.when(pos < depth - 1)
                def _():
                    self.held[stream, c] = value.astype(BF16)
                    self.up(stream, c, self.held.at[stream, c], ahead).start()

                @pl.when(pos == depth - 1)
                def _():
                    self.out[self.place(stream, c), :] = value.astype(BF16)
                    self.down(stream, c, behind).start()

            b = t - lag * (2 * depth - 3 - pos)

            @pl.when((b >= 0) & (b < self.chunks) & (pos < depth - 1))
            def _():
                self.down(stream, b, self.h).wait_recv()

                @pl.when(pos > 0)
                def _():
                    self.down(stream, b, behind).start()

    def run(self, start, stop):
        def one(t, carry):
            self.step(t)
            return carry

        lax.fori_loop(start, stop, one, 0)

    def drain(self):
        def one(c, carry):
            for stream in range(2):
                pos, ahead, behind = self.ends(stream)

                @pl.when(pos < self.depth - 1)
                def _():
                    self.up(stream, c, self.held.at[stream, c], self.h).wait_send()

                @pl.when(pos > 0)
                def _():
                    self.down(stream, c, self.h).wait_send()

            return carry

        lax.fori_loop(0, self.chunks, one, 0)


class Across:
    def __init__(self, depth, part, others, send_sem, recv_sem):
        self.depth, self.part, self.others, self.sems = depth, part, others, (send_sem, recv_sem)
        self.h = lax.axis_index("heads")

    def copy(self, d):
        to = lax.rem(self.h + d, self.depth)
        return remote(
            self.part, self.others.at[self.h], self.sems[0].at[d], self.sems[1].at[self.h], heads=to
        )

    def start(self):
        for d in range(1, self.depth):
            self.copy(d).start()

    def finish(self):
        value = self.part[...].astype(F32)
        for d in range(1, self.depth):
            came = self.others.at[lax.rem(self.h + d, self.depth)]
            pltpu.make_async_copy(came, came, self.sems[1].at[lax.rem(self.h + d, self.depth)]).wait()
            value = value + came[...].astype(F32)
        for d in range(1, self.depth):
            self.copy(d).wait_send()
        return value


def column_stats(w, at, b, aw):
    ab = dot(dot(at, at, NT), b)
    bf = b.astype(F32)

    def square(rows, acc):
        v = w[rows, :].astype(F32)
        return acc + fold(v * v)

    acc = row_loop(w.shape[0], 128, square, jnp.zeros((8, w.shape[1]), F32))
    squares = total(acc) + 2.0 * ADAPT_SCALE * total(bf * aw) + ADAPT_SCALE**2 * total(bf * ab)
    return squares, aw + ADAPT_SCALE * ab


def front_kernel(
    seq_n, depth, rows_n, group, heads,
    x, gain, cos, sin, at_qkv, b_qkv, m_qkv, at_out, b_out, at_down, b_down, at_gu, b_gu,
    w_qkv, w_out, w_down, w_gu,
    q, k, v, h1, pre, low, norm_qkv, v_qkv, norms, v_out, v_down, norm_gu, v_gu,
    wq, wo, wd, wg, turned, part, others, q_send, q_recv, k_send, k_recv, v_send, v_recv, z_send, z_recv, load,
):
    count, pairs = rows_n * group, rows_n * heads
    loads = [pltpu.make_async_copy(w_qkv.at[i], wq.at[i], load.at[i]) for i in range(3)]
    loads += [
        pltpu.make_async_copy(w_out, wo, load.at[3]),
        pltpu.make_async_copy(w_down, wd, load.at[4]),
        pltpu.make_async_copy(w_gu, wg, load.at[5]),
    ]
    for one in loads:
        one.start()
    greet(seq=seq_n, heads=depth)

    def norm(rows, carry):
        v = x[rows, :].astype(F32)
        inverse = lax.rsqrt(jnp.mean(v * v, axis=-1, keepdims=True) + NORM_EPS)
        h1[rows, :] = (v * inverse * gain[...]).astype(BF16)
        return carry

    row_loop(count, 32, norm)
    for i in range(3):
        h1[count + i * RANK : count + (i + 1) * RANK, :] = at_qkv[i]
    for i in range(3):
        low[i] = dot(h1[:count, :], at_qkv[i], NT).astype(BF16)
    exchanges = [
        Exchange(kind, seq_n, pairs, lambda j, i=i: turned.at[i, j], lambda j, to=to: to.at[j], *sems)
        for i, (kind, to, sems) in enumerate(
            (("queries", q, (q_send, q_recv)), ("keys", k, (k_send, k_recv)), ("keys", v, (v_send, v_recv)))
        )
    ]
    for i in range(3):
        loads[i].wait()

        def project(over, t, i=i):
            width = over.size
            r = dot(h1[...], wq[i, :, over])
            b = b_qkv[i, :, over]
            value = r[:count] + ADAPT_SCALE * dot(low[i], b)
            aw = r[count + i * RANK : count + (i + 1) * RANK]
            squares, av = column_stats(wq.at[i, :, over], at_qkv[i], b, aw)
            n = jnp.sqrt(squares + COLUMN_EPS)
            norm_qkv[i : i + 1, over] = n
            v_qkv[i, :, over] = av
            pre[i, :, over] = value.astype(BF16)
            scaled = value * (m_qkv[i : i + 1, over] / n)
            for row in range(rows_n):
                rows = slice(row * group, (row + 1) * group)
                for hh in range(width // HD):
                    part_ = scaled[rows, hh * HD : (hh + 1) * HD]
                    if i < 2:
                        part_ = part_ * cos[rows, :] + pltpu.roll(part_, HD // 2, 1) * sin[rows, :]
                    turned[i, row * heads + t * (width // HD) + hh] = part_.astype(BF16)

        tiles(heads * HD, 256, project)
        exchanges[i].start()

    part[...] = jnp.zeros_like(part)
    for row, (w, at, b, av, loaded) in enumerate(
        ((wo, at_out, b_out, v_out, loads[3]), (wd, at_down, b_down, v_down, loads[4]))
    ):
        loaded.wait()

        def stats(over, t, row=row, w=w, at=at, b=b, av=av):
            squares, value = column_stats(w.at[:, over], at[...], b[:, over], dot(at[...], w[:, over]))
            part[row : row + 1, over] = squares
            av[:, over] = value

        tiles(w.shape[1], 256, stats)
    across = Across(depth, part, others, z_send, z_recv)
    across.start()
    loads[5].wait()
    for i in range(2):

        def stats_gu(over, t, i=i):
            b = b_gu[i, :, over]
            squares, value = column_stats(wg.at[i, :, over], at_gu[i], b, dot(at_gu[i], wg[i, :, over]))
            norm_gu[i : i + 1, over] = jnp.sqrt(squares + COLUMN_EPS)
            v_gu[i, :, over] = value

        tiles(wg.shape[2], 256, stats_gu)
    norms[...] = jnp.sqrt(across.finish() + COLUMN_EPS)
    for one in exchanges:
        one.wait_recv()
    for one in exchanges:
        one.wait_send()


def front(sizes, x, gain, cos, sin, qkv, out, down, gu):
    seq_n, depth, rows_n, group, heads = sizes
    count, pairs, width = rows_n * group, rows_n * heads, x.shape[1]
    local, hidden = qkv[0].shape[2], gu[0].shape[2]
    return pl.pallas_call(
        functools.partial(front_kernel, *sizes),
        out_shape=[
            shape(pairs, group, HD), shape(seq_n, group, HD), shape(seq_n, group, HD),
            shape(count + 3 * RANK, width), shape(3, count, local), shape(3, count, RANK),
            shape(3, local, dtype=F32), shape(3, RANK, local, dtype=F32), shape(8, width, dtype=F32),
            shape(RANK, width, dtype=F32), shape(RANK, width, dtype=F32),
            shape(2, hidden, dtype=F32), shape(2, RANK, hidden, dtype=F32),
        ],
        in_specs=[IN_VMEM] * 13 + [ANYWHERE] * 4,
        out_specs=[IN_VMEM] * 13,
        scratch_shapes=[
            pltpu.VMEM(qkv[0].shape, BF16), pltpu.VMEM(out[0].shape, BF16), pltpu.VMEM(down[0].shape, BF16),
            pltpu.VMEM(gu[0].shape, BF16), pltpu.VMEM((3, pairs, group, HD), BF16),
            pltpu.VMEM((8, width), F32), pltpu.VMEM((depth, 8, width), F32),
            dma(pairs), dma(pairs), dma(seq_n), dma(seq_n), dma(seq_n), dma(seq_n), dma(depth), dma(depth), dma(6),
        ],
        compiler_params=params(56, 1),
    )(
        x, gain, cos, sin, qkv[1], qkv[2], qkv[3], out[1], out[2], down[1], down[2], gu[1], gu[2],
        qkv[0], out[0], down[0], gu[0],
    )


def attend_kernel(block, low_ref, high_ref, q_ref, k_ref, v_ref, start_ref, place_ref, o_ref, lse_ref, vt):
    scale = HD**-0.5
    vt[...] = v_ref[...].T

    def per_query(i, carry):
        at = pl.ds(pl.multiple_of(i * block, block), block)
        q = q_ref[at, :]
        start, place = start_ref[:, at], place_ref[:, at]

        def per_key(j, state):
            top, count, acc = state
            over = pl.ds(pl.multiple_of(j * block, block), block)
            s = dot(k_ref[over, :], q, NT) * scale
            key = j * block + lax.broadcasted_iota(jnp.int32, (block, block), 0)
            s = jnp.where((key >= start) & (key <= place), s, NEG_LARGE)
            new_top = jnp.maximum(top, jnp.max(s, axis=0, keepdims=True))
            p = jnp.exp(s - new_top)
            fade = jnp.exp(top - new_top)
            count = count * fade + total(p)
            acc = acc * fade + dot(vt[:, over], p)
            return new_top, count, acc

        begin = (
            jnp.full((1, block), -1e29, F32),
            jnp.zeros((1, block), F32),
            jnp.zeros((HD, block), F32),
        )
        top, count, acc = lax.fori_loop(low_ref[i], high_ref[i] + 1, per_key, begin)
        o_ref[at, :] = (acc / count).T.astype(BF16)
        lse_ref[:, at] = top + jnp.log(count)
        return carry

    lax.fori_loop(0, q_ref.shape[0] // block, per_query, 0)


def attend(q, k, v, low, high, start, place, block):
    return pl.pallas_call(
        functools.partial(attend_kernel, block),
        out_shape=[shape(*q.shape), shape(1, q.shape[0], dtype=F32)],
        in_specs=[IN_SMEM] * 2 + [IN_VMEM] * 5,
        out_specs=[IN_VMEM] * 2,
        scratch_shapes=[pltpu.VMEM((HD, k.shape[0]), BF16)],
        compiler_params=params(24),
    )(low, high, q, k, v, start, place)


def attend_back_kernel(
    block, low_ref, high_ref, q_ref, k_ref, v_ref, o_ref, do_ref, lse_ref, start_ref, place_ref,
    dq_ref, dk_ref, dv_ref, kt, dk_acc, dv_acc,
):
    scale = HD**-0.5
    kt[...] = k_ref[...].T
    dk_acc[...] = jnp.zeros_like(dk_acc)
    dv_acc[...] = jnp.zeros_like(dv_acc)

    def per_query(i, carry):
        at = pl.ds(pl.multiple_of(i * block, block), block)
        q, do = q_ref[at, :], do_ref[at, :]
        start, place, lse = start_ref[:, at], place_ref[:, at], lse_ref[:, at]
        delta = total((do.astype(F32) * o_ref[at, :].astype(F32)).T)

        def per_key(j, acc):
            over = pl.ds(pl.multiple_of(j * block, block), block)
            k = k_ref[over, :]
            s = dot(k, q, NT) * scale
            key = j * block + lax.broadcasted_iota(jnp.int32, (block, block), 0)
            p = jnp.exp(jnp.where((key >= start) & (key <= place), s - lse, NEG_LARGE))
            dp = dot(v_ref[over, :], do, NT)
            ds = (p * (dp - delta)).astype(BF16)
            dv_acc[over, :] += dot(p, do)
            dk_acc[over, :] += dot(ds, q)
            return acc + dot(kt[:, over], ds)

        acc = lax.fori_loop(low_ref[i], high_ref[i] + 1, per_key, jnp.zeros((HD, block), F32))
        dq_ref[at, :] = (acc * scale).T.astype(BF16)
        return carry

    lax.fori_loop(0, q_ref.shape[0] // block, per_query, 0)
    dk_ref[...] = (dk_acc[...] * scale).astype(BF16)
    dv_ref[...] = dv_acc[...].astype(BF16)


def attend_back(q, k, v, o, do, lse, low, high, start, place, block):
    return pl.pallas_call(
        functools.partial(attend_back_kernel, block),
        out_shape=[shape(*a.shape) for a in (q, k, v)],
        in_specs=[IN_SMEM] * 2 + [IN_VMEM] * 8,
        out_specs=[IN_VMEM] * 3,
        scratch_shapes=[
            pltpu.VMEM((HD, k.shape[0]), BF16), pltpu.VMEM(k.shape, F32), pltpu.VMEM(v.shape, F32)
        ],
        compiler_params=params(24),
    )(low, high, q, k, v, o, do, lse, start, place)


def out_kernel(
    seq_n, depth, rows_n, group, heads, o, w, at, b, out, attn, low, part, send, recv, *line_refs
):
    greet(seq=seq_n, line=depth)

    def landing(pair):
        row, head = pair // heads, lax.rem(pair, heads)
        return attn.at[
            pl.ds(pl.multiple_of(row * group, group), group), pl.ds(pl.multiple_of(head * HD, HD), HD)
        ]

    exchange = Exchange("queries_back", seq_n, rows_n * heads, lambda i: o.at[i], landing, send, recv)
    exchange.start()
    exchange.wait_recv()
    low[...] = dot(attn[...], at[...], NT).astype(BF16)

    def project(over, t):
        part[:, over] = (dot(attn[...], w[:, over]) + ADAPT_SCALE * dot(low[...], b[:, over])).astype(BF16)

    tiles(w.shape[1], 256, project)
    line = Line(depth, part, out, *line_refs)
    line.first()
    line.run(0, line.steps)
    line.drain()
    exchange.wait_send()


def out_project(sizes, o, w, at, b):
    seq_n, depth, rows_n, group, heads = sizes
    count, pairs, width = rows_n * group, rows_n * heads, w.shape[1]
    return pl.pallas_call(
        functools.partial(out_kernel, *sizes),
        out_shape=[shape(count, width), shape(count, heads * HD), shape(count, RANK)],
        in_specs=[IN_VMEM] * 4,
        out_specs=[IN_VMEM] * 3,
        scratch_shapes=[pltpu.VMEM((count, width), BF16), dma(pairs), dma(pairs)]
        + Line.scratch(count, width, 32),
        compiler_params=params(24, 2),
    )(o, w, at, b)


def ffn_kernel(
    out_pre, x, m_out, norms, gain, at_gu, b_gu, m_gu, norm_gu, v_gu, at_down, b_down, m_down, cotangent,
    w_gu, w_down,
    dh2, down_part, s_down, ga_gu, gb_gu, gm_gu, g_gain, ga_down, gb_down,
    wg, wd, h2, pre, z, dp, dpd, tmp, low, load,
):
    count = x.shape[0]
    hidden, width = wg.shape[2], wd.shape[1]
    loads = [pltpu.make_async_copy(w_gu.at[i], wg.at[i], load.at[i]) for i in range(2)]
    loads.append(pltpu.make_async_copy(w_down, wd, load.at[2]))
    for one in loads:
        one.start()
    c_out = m_out[...] / norms[0:1, :]
    c_down = m_down[...] / norms[1:2, :]

    def norm(rows, carry):
        x2 = x[rows, :].astype(F32) + out_pre[rows, :].astype(F32) * c_out
        inverse = lax.rsqrt(jnp.mean(x2 * x2, axis=-1, keepdims=True) + NORM_EPS)
        h2[rows, :] = (x2 * inverse * gain[...]).astype(BF16)
        dpd[rows, :] = (cotangent[rows, :].astype(F32) * c_down).astype(BF16)
        return carry

    row_loop(count, 32, norm)
    for i in range(2):
        low[i] = dot(h2[...], at_gu[i], NT).astype(BF16)
    loads[0].wait()
    loads[1].wait()

    def forward(over, t):
        n = over.size
        for i in range(2):
            tmp[i, :, :n] = dot(h2[...], wg[i, :, over]) + ADAPT_SCALE * dot(low[i], b_gu[i, :, over])
        scale = [m_gu[i : i + 1, over] / norm_gu[i : i + 1, over] for i in range(2)]

        def gated(rows, carry):
            g, u = tmp[0, rows, :n], tmp[1, rows, :n]
            pre[0, rows, over] = g.astype(BF16)
            pre[1, rows, over] = u.astype(BF16)
            g = g * scale[0]
            z[rows, over] = (g * jax.nn.sigmoid(g) * (u * scale[1])).astype(BF16)
            return carry

        row_loop(count, 64, gated)

    tiles(hidden, 256, forward)
    loads[2].wait()
    low_down = dot(z[...], at_down[...], NT).astype(BF16)
    s_down[...] = jnp.zeros_like(s_down)

    def down(over, t):
        value = dot(z[...], wd[:, over]) + ADAPT_SCALE * dot(low_down, b_down[:, over])
        down_part[:, over] = value.astype(BF16)
        s_down[0:1, over] = total(value * cotangent[:, over].astype(F32))
        gb_down[:, over] = ADAPT_SCALE * dot(low_down, dpd[:, over], TN)

    tiles(width, 256, down)
    dlow_down = (ADAPT_SCALE * dot(dpd[...], b_down[...], NT)).astype(BF16)

    def backward(over, t):
        n = over.size
        tmp[0, :, :n] = dot(dpd[...], wd[over, :], NT) + dot(dlow_down, at_down[:, over])
        ga_down[:, over] = dot(dlow_down, z[:, over], TN)
        scale = [m_gu[i : i + 1, over] / norm_gu[i : i + 1, over] for i in range(2)]

        def gated(rows, sums):
            dz = tmp[0, rows, :n]
            pg, pu = pre[0, rows, over].astype(F32), pre[1, rows, over].astype(F32)
            g, u = pg * scale[0], pu * scale[1]
            sigma = jax.nn.sigmoid(g)
            e_g = dz * u * sigma * (1.0 + g * (1.0 - sigma))
            e_u = dz * g * sigma
            dp[0, rows, over] = (e_g * scale[0]).astype(BF16)
            dp[1, rows, over] = (e_u * scale[1]).astype(BF16)
            return sums[0] + fold(e_g * pg), sums[1] + fold(e_u * pu)

        zero = jnp.zeros((8, n), F32)
        sums = row_loop(count, 64, gated, (zero, zero))
        for i in range(2):
            s, inverse = total(sums[i]), 1.0 / norm_gu[i : i + 1, over]
            gm_gu[i : i + 1, over] = s * inverse
            turn = m_gu[i : i + 1, over] * s * inverse * inverse * inverse
            dp[i, count : count + RANK, over] = (b_gu[i, :, over].astype(F32) * turn).astype(BF16)
            gb_gu[i, :, over] = ADAPT_SCALE * (
                dot(low[i], dp[i, :count, over], TN) - v_gu[i, :, over] * turn
            )

    tiles(hidden, 256, backward)
    both = [dot(dp[i], b_gu[i], NT) for i in range(2)]
    dlow = [(ADAPT_SCALE * both[i][:count]).astype(BF16) for i in range(2)]
    turned = [both[i][count:] for i in range(2)]

    def inputs(over, t):
        r = [dot(dp[i], wg[i, over, :], NT) for i in range(2)]
        value = r[0][:count] + r[1][:count]
        for i in range(2):
            value = value + dot(dlow[i], at_gu[i, :, over])
            v_tb = r[i][count:] + ADAPT_SCALE * dot(turned[i], at_gu[i, :, over])
            ga_gu[i, :, over] = dot(dlow[i], h2[:, over], TN) - ADAPT_SCALE * v_tb
        dh2[:, over] = value.astype(BF16)
        g_gain[:, over] = total(value * h2[:, over].astype(F32)) / gain[:, over]

    tiles(width, 256, inputs)


def ffn(out_pre, x, m_out, norms, gain, gu, m_gu, norm_gu, v_gu, down, m_down, cotangent):
    count, width = x.shape
    hidden = gu[0].shape[2]
    return pl.pallas_call(
        ffn_kernel,
        out_shape=[
            shape(count, width), shape(count, width), shape(8, width, dtype=F32),
            shape(2, RANK, width, dtype=F32), shape(2, RANK, hidden, dtype=F32), shape(2, hidden, dtype=F32),
            shape(1, width, dtype=F32), shape(RANK, hidden, dtype=F32), shape(RANK, width, dtype=F32),
        ],
        in_specs=[IN_VMEM] * 14 + [ANYWHERE] * 2,
        out_specs=[IN_VMEM] * 9,
        scratch_shapes=[
            pltpu.VMEM(gu[0].shape, BF16), pltpu.VMEM(down[0].shape, BF16), pltpu.VMEM((count, width), BF16),
            pltpu.VMEM((2, count, hidden), BF16), pltpu.VMEM((count, hidden), BF16),
            pltpu.VMEM((2, count + RANK, hidden), BF16), pltpu.VMEM((count, width), BF16),
            pltpu.VMEM((2, count, 256), F32), pltpu.VMEM((2, count, RANK), BF16), dma(3),
        ],
        compiler_params=params(60),
    )(
        out_pre, x, m_out, norms, gain, gu[1], gu[2], m_gu, norm_gu, v_gu, down[1], down[2], m_down,
        cotangent, gu[0], down[0],
    )


def middle_kernel(depth, x, s_part, out, s_out, others, z_send, z_recv, *line_refs):
    greet(heads=depth)
    across = Across(depth, s_part, others, z_send, z_recv)
    line = Line(depth, x, out, *line_refs)
    across.start()
    line.first()
    line.run(0, line.steps)
    line.drain()
    s_out[...] = across.finish()


def middle(sizes, x, s_part):
    depth = sizes[1]
    count, width = x.shape
    return pl.pallas_call(
        functools.partial(middle_kernel, depth),
        out_shape=[shape(count, width), shape(8, width, dtype=F32)],
        in_specs=[IN_VMEM] * 2,
        out_specs=[IN_VMEM] * 2,
        scratch_shapes=[pltpu.VMEM((depth, 8, width), F32), dma(depth), dma(depth)]
        + Line.scratch(count, width, 32),
        compiler_params=params(20, 3),
    )(x, s_part)


def out_back_kernel(
    seq_n, depth, rows_n, group, heads,
    dh2, x, out_pre, cotangent, gain, m_out, norms, w, at, b, v_out, attn, low,
    do, dx2, ga, gb, gm, dp, blocks, send, recv,
):
    count = rows_n * group
    greet(seq=seq_n)
    inverse_n = 1.0 / norms[0:1, :]
    c = m_out[...] * inverse_n

    def back(rows, sums):
        pre = out_pre[rows, :].astype(F32)
        x2 = x[rows, :].astype(F32) + pre * c
        inverse = lax.rsqrt(jnp.mean(x2 * x2, axis=-1, keepdims=True) + NORM_EPS)
        scaled = dh2[rows, :].astype(F32) * gain[...]
        mean = jnp.mean(scaled * x2, axis=-1, keepdims=True)
        e = cotangent[rows, :].astype(F32) + inverse * scaled - x2 * (inverse**3 * mean)
        dx2[rows, :] = e.astype(BF16)
        dp[rows, :] = (e * c).astype(BF16)
        return sums + fold(e * pre)

    s = total(row_loop(count, 16, back, jnp.zeros((8, x.shape[1]), F32)))
    turn = m_out[...] * s * inverse_n * inverse_n * inverse_n
    gm[...] = s * inverse_n
    dp[count : count + RANK, :] = (b[...].astype(F32) * turn).astype(BF16)
    both = dot(dp[...], b[...], NT)
    dlow, turned = (ADAPT_SCALE * both[:count]).astype(BF16), both[count:]
    exchange = Exchange(
        "queries", seq_n, rows_n * heads, lambda p: blocks.at[p], lambda s_: do.at[s_], send, recv
    )

    def inputs(over, t):
        r = dot(dp[...], w[over, :], NT)
        value = (r[:count] + dot(dlow, at[:, over])).astype(BF16)
        for row in range(rows_n):
            for hh in range(over.size // HD):
                blocks[row * heads + t * (over.size // HD) + hh] = value[
                    row * group : (row + 1) * group, hh * HD : (hh + 1) * HD
                ]
        ga[:, over] = dot(dlow, attn[:, over], TN) - ADAPT_SCALE * (
            r[count:] + ADAPT_SCALE * dot(turned, at[:, over])
        )

    tiles(heads * HD, 256, inputs)
    exchange.start()

    gb[...] = ADAPT_SCALE * (dot(low[...], dp[:count, :], TN) - v_out[...] * turn)
    exchange.wait_recv()
    exchange.wait_send()


def out_back(sizes, dh2, x, out_pre, cotangent, gain, m_out, norms, w, at, b, v_out, attn, low):
    seq_n, depth, rows_n, group, heads = sizes
    count, pairs, width = rows_n * group, rows_n * heads, x.shape[1]
    return pl.pallas_call(
        functools.partial(out_back_kernel, *sizes),
        out_shape=[
            shape(pairs, group, HD), shape(count, width), shape(RANK, heads * HD, dtype=F32),
            shape(RANK, width, dtype=F32), shape(1, width, dtype=F32),
        ],
        in_specs=[IN_VMEM] * 13,
        out_specs=[IN_VMEM] * 5,
        scratch_shapes=[
            pltpu.VMEM((count + RANK, width), BF16), pltpu.VMEM((pairs, group, HD), BF16), dma(pairs), dma(pairs)
        ],
        compiler_params=params(40, 4),
    )(dh2, x, out_pre, cotangent, gain, m_out, norms, w, at, b, v_out, attn, low)


def last_kernel(
    seq_n, depth, rows_n, group, heads,
    dq, dk, dv, cos, sin, h1, pre, low, gain, at, b, m, norm, v_qkv,
    ga_gu, gb_out, gb_down, g_gain2, gm_out, s_down, ga_out, gb_gu, gm_gu, ga_down,
    m_down, norms, at_down, b_down, v_down, w_qkv, w_down,
    dh1, wide, local, hid,
    wq, wd, gq, gk, gv, dp, part, wide_in, local_in, hid_in, wide_got, local_got, hid_got,
    piece, pieces, done, q_send, q_recv, k_send, k_recv, v_send, v_recv, load,
    r_send, r_recv, g_send, g_recv, z_send, z_recv, *line_refs,
):
    count, pairs, width = rows_n * group, rows_n * heads, h1.shape[1]
    fan, me = seq_n // pairs, lax.axis_index("seq")
    loads = [pltpu.make_async_copy(w_qkv, wq, load.at[0]), pltpu.make_async_copy(w_down, wd, load.at[1])]
    for one in loads:
        one.start()
    greet(seq=seq_n, heads=depth)
    exchanges = [
        Exchange(kind, seq_n, pairs, lambda j, a=a: a.at[j], lambda j, to=to: to.at[j], *sems)
        for kind, a, to, sems in (
            ("queries_back", dq, gq, (q_send, q_recv)),
            ("keys_back", dk, gk, (k_send, k_recv)),
            ("keys_back", dv, gv, (v_send, v_recv)),
        )
    ]
    for one in exchanges:
        one.start()

    wide_in[...] = jnp.zeros_like(wide_in)
    local_in[...] = jnp.zeros_like(local_in)
    hid_in[...] = jnp.zeros_like(hid_in)
    inverse_n = 1.0 / norms[1:2, :]
    s = s_down[0:1, :]
    turn = m_down[...] * s * inverse_n * inverse_n * inverse_n
    tb = (b_down[...].astype(F32) * turn).astype(BF16)
    loads[1].wait()
    v_tb = ADAPT_SCALE * dot(dot(tb, b_down[...], NT), at_down[...])
    share = 1.0 / depth
    for i in range(2):
        wide_in[(3 + i) * RANK : (4 + i) * RANK, :] = ga_gu[i].astype(BF16)
        hid_in[i * RANK : (i + 1) * RANK, :] = gb_gu[i].astype(BF16)
    wide_in[5 * RANK : 6 * RANK, :] = gb_out[...].astype(BF16)
    wide_in[6 * RANK : 7 * RANK, :] = (gb_down[...] - ADAPT_SCALE * v_down[...] * turn).astype(BF16)
    hid_in[3 * RANK : 4 * RANK, :] = (ga_down[...] - ADAPT_SCALE * (v_tb + dot(tb, wd[...], NT))).astype(BF16)
    local_in[4 * RANK : 5 * RANK, :] = ga_out[...].astype(BF16)
    hid_in[2 * RANK : 3 * RANK, :] = jnp.concatenate(
        [gm_gu[...], jnp.zeros((RANK - 2, hid_in.shape[1]), F32)], axis=0
    ).astype(BF16)

    sums = [None] * 3
    loads[0].wait()
    for i in range(3):
        exchanges[i].wait_recv()
        came = (gq, gk, gv)[i]
        for head in range(heads):
            cols = slice(head * HD, (head + 1) * HD)
            n = norm[i : i + 1, cols]
            c = m[i : i + 1, cols] / n
            s = jnp.zeros((1, HD), F32)
            for row in range(rows_n):
                rows = slice(row * group, (row + 1) * group)
                if i == 0:
                    e = came[row * heads + head].astype(F32)
                else:
                    e = came[(row * heads + head) * fan].astype(F32)
                    for g in range(1, fan):
                        e = e + came[(row * heads + head) * fan + g].astype(F32)
                if i < 2:
                    e = e * cos[rows, :] - pltpu.roll(e, HD // 2, 1) * sin[rows, :]
                s = s + total(e * pre[i, rows, cols].astype(F32))
                dp[i, rows, cols] = (e * c).astype(BF16)
            turn = m[i : i + 1, cols] * s / (n * n * n)
            dp[i, count : count + RANK, cols] = (b[i, :, cols].astype(F32) * turn).astype(BF16)
            local_in[i * RANK : (i + 1) * RANK, cols] = (
                ADAPT_SCALE * (dot(low[i], dp[i, :count, cols], TN) - v_qkv[i, :, cols] * turn)
            ).astype(BF16)
            sums[i] = [s / n] if head == 0 else sums[i] + [s / n]
    local_in[3 * RANK : 4 * RANK, :] = jnp.concatenate(
        [jnp.concatenate(one, axis=1) for one in sums]
        + [jnp.zeros((RANK - 3, heads * HD), F32)], axis=0
    ).astype(BF16)
    both = [dot(dp[i], b[i], NT) for i in range(3)]
    dlow = [(ADAPT_SCALE * both[i][:count]).astype(BF16) for i in range(3)]
    turned = [both[i][count:] for i in range(3)]

    def inputs(over, t):
        value = jnp.zeros((count, over.size), F32)
        for i in range(3):
            r = dot(dp[i], wq[i, over, :], NT)
            value = value + r[:count] + dot(dlow[i], at[i, :, over])
            wide_in[i * RANK : (i + 1) * RANK, over] = (
                dot(dlow[i], h1[:count, over], TN)
                - ADAPT_SCALE * (r[count:] + ADAPT_SCALE * dot(turned[i], at[i, :, over]))
            ).astype(BF16)
        part[:, over] = value.astype(BF16)
        g_gain1 = total(value * h1[:count, over].astype(F32)) / gain[:, over]
        wide_in[7 * RANK : 8 * RANK, over] = jnp.concatenate(
            [
                g_gain1, g_gain2[:, over], gm_out[:, over] * share,
                s_down[0:1, over] / norms[1:2, over] * share,
                jnp.zeros((RANK - 4, over.size), F32),
            ], axis=0,
        ).astype(BF16)

    tiles(width, 256, inputs)
    line = Line(depth, part, dh1, *line_refs)
    line.first()

    spread = seq_n // OWNERS
    slabs = (
        (wide_in, wide_got, wide, lambda j: j), (local_in, local_got, local, lambda j: j),
        (hid_in, hid_got, hid, lambda j: OWNERS - 1 - j),
    )
    own = me // spread
    chosen = lax.rem(me, spread) == 0

    def rows_of(j):
        return pl.ds(pl.multiple_of(j * RANK, RANK), RANK)

    def to_owner(i, j):
        src, got, _, owner = slabs[i]
        return remote(
            src.at[rows_of(j)], got.at[me], r_send.at[i, j], r_recv.at[i, me], seq=owner(j) * spread
        )

    def from_owner(i, j, target):
        result = slabs[i][2]
        return remote(
            done.at[i, :, : result.shape[1]], result.at[rows_of(j)], g_send.at[i, target], g_recv.at[i, j], seq=target
        )

    for i, (src, got, result, owner) in enumerate(slabs):
        for j in range(src.shape[0] // RANK):

            @pl.when(me != owner(j) * spread)
            def _(i=i, j=j):
                to_owner(i, j).start()

            @pl.when(me == owner(j) * spread)
            def _(src=src, got=got, i=i, j=j):
                pltpu.make_async_copy(src.at[rows_of(j)], got.at[me], r_recv.at[i, me]).start()

    line.run(0, 4)
    across = Across(depth, piece, pieces, z_send, z_recv)
    blocks_n = [slab[0].shape[0] // RANK for slab in slabs]
    owns = [chosen & (slab[3](own) < n) for slab, n in zip(slabs, blocks_n)]
    for i, (src, got, result, owner) in enumerate(slabs):

        @pl.when(owns[i])
        def _(i=i, got=got, result=result):
            def add(s_, acc):
                pltpu.make_async_copy(got.at[s_], got.at[s_], r_recv.at[i, s_]).wait()
                return acc + got[s_].astype(F32)

            value = lax.fori_loop(0, seq_n, add, jnp.zeros((RANK, result.shape[1]), F32))
            if i == 0:
                piece[...] = value.astype(BF16)
                across.start()
            else:
                done[i, :, : result.shape[1]] = value.astype(BF16)

    line.run(4, 8)

    @pl.when(owns[0])
    def _():
        done[0, :, :] = across.finish().astype(BF16)

    for i, (src, got, result, owner) in enumerate(slabs):

        @pl.when(owns[i])
        def _(i=i, result=result, owner=owner):
            mine = owner(own)

            def give(d, carry):
                from_owner(i, mine, lax.rem(me + d, seq_n)).start()
                return carry

            lax.fori_loop(1, seq_n, give, 0)
            pltpu.make_async_copy(
                done.at[i, :, : result.shape[1]], result.at[rows_of(mine)], g_recv.at[i, mine]
            ).start()

    line.run(8, line.steps)
    line.drain()
    for one in exchanges:
        one.wait_send()
    for i, (src, got, result, owner) in enumerate(slabs):
        for j in range(blocks_n[i]):

            @pl.when(me != owner(j) * spread)
            def _(i=i, j=j):
                to_owner(i, j).wait_send()

            pltpu.make_async_copy(result.at[rows_of(j)], result.at[rows_of(j)], g_recv.at[i, j]).wait()

        @pl.when(owns[i])
        def _(i=i, owner=owner):
            def given(d, carry):
                from_owner(i, owner(own), lax.rem(me + d, seq_n)).wait_send()
                return carry

            lax.fori_loop(1, seq_n, given, 0)


def last(sizes, ins, qkv_w, w_down):
    seq_n, depth, rows_n, group, heads = sizes
    count, pairs, width = rows_n * group, rows_n * heads, w_down.shape[1]
    local, hidden = qkv_w.shape[2], w_down.shape[0]
    blocks = {width: 8, local: 5, hidden: 4}
    slabs = [(n * RANK, w) for w, n in blocks.items()]
    return pl.pallas_call(
        functools.partial(last_kernel, *sizes),
        out_shape=[shape(count, width)] + [shape(*s) for s in slabs],
        in_specs=[IN_VMEM] * len(ins) + [ANYWHERE] * 2,
        out_specs=[IN_VMEM] * 4,
        scratch_shapes=[
            pltpu.VMEM(qkv_w.shape, BF16), pltpu.VMEM(w_down.shape, BF16),
            pltpu.VMEM((pairs, group, HD), BF16), pltpu.VMEM((seq_n, group, HD), BF16),
            pltpu.VMEM((seq_n, group, HD), BF16), pltpu.VMEM((3, count + RANK, local), BF16),
            pltpu.VMEM((count, width), BF16),
        ]
        + [pltpu.VMEM(s, BF16) for s in slabs]
        + [pltpu.VMEM((seq_n, RANK, s[1]), BF16) for s in slabs]
        + [
            pltpu.VMEM((RANK, width), BF16), pltpu.VMEM((depth, RANK, width), BF16), pltpu.VMEM((3, RANK, width), BF16),
            dma(pairs), dma(pairs), dma(seq_n), dma(seq_n), dma(seq_n), dma(seq_n), dma(2),
            dma(3, 8), dma(3, seq_n), dma(3, seq_n), dma(3, 8), dma(depth), dma(depth),
        ]
        + Line.scratch(count, width, 32),
        compiler_params=params(60, 5),
    )(*ins, qkv_w, w_down)


def per_device(
    tokens, attn_gain, base_qkv, adapt_a_qkv, adapt_b_qkv, magnitude_qkv, base_out, adapt_a_out,
    adapt_b_out, magnitude_out, ffn_gain, base_gu, adapt_a_gu, adapt_b_gu, magnitude_gu, base_down,
    adapt_a_down, adapt_b_down, magnitude_down, doc_lengths, cotangent,
):
    rows_n, group, width = tokens.shape
    count = rows_n * group
    local = base_qkv.shape[2]
    heads = local // HD
    pairs = rows_n * heads
    seq_n, depth = lax.axis_size("seq"), lax.axis_size("heads")
    sizes = (seq_n, depth, rows_n, group, heads)
    fan = seq_n // pairs
    length = group * seq_n
    me = lax.axis_index("seq")

    order = jnp.arange(doc_lengths.shape[1])
    doc_ends = jnp.sum(
        jnp.where(order[None, :, None] <= order[None, None, :], doc_lengths[:, :, None], 0), axis=1
    )
    doc_starts = doc_ends - doc_lengths

    def starts_of(places, ends, starts):
        inside = (places[..., None] >= starts) & (places[..., None] < ends)
        return jnp.sum(jnp.where(inside, starts, 0), axis=-1)

    mine = me * group + jnp.arange(group, dtype=jnp.int32)
    position = mine[None, :] - starts_of(
        jnp.broadcast_to(mine[None, :], (rows_n, group)), doc_ends[:, None], doc_starts[:, None]
    )
    half = HD // 2
    frequency = ROPE_BASE ** (jnp.arange(half, dtype=F32) * (-2.0 / HD))
    angles = position.reshape(count, 1).astype(F32) * frequency
    cos, sin = jnp.cos(angles), jnp.sin(angles)
    cos, sin = jnp.concatenate([cos, cos], axis=1), jnp.concatenate([-sin, sin], axis=1)
    row = me // fan // heads
    block_at = lax.rem(me, fan) + fan * jnp.arange(pairs, dtype=jnp.int32)
    place = (block_at[:, None] * group + jnp.arange(group, dtype=jnp.int32)[None, :]).reshape(-1)
    pick = (jnp.arange(rows_n) == row)[:, None]
    row_ends = jnp.sum(jnp.where(pick, doc_ends, 0), axis=0)
    row_starts = jnp.sum(jnp.where(pick, doc_starts, 0), axis=0)
    start = starts_of(place, row_ends, row_starts)
    low_block = start.reshape(-1, group)[:, 0] // group
    place, start = place[None, :], start[None, :]

    x = tokens.reshape(count, width)
    dy = cotangent.reshape(count, width)
    gain1, gain2 = attn_gain[None, :], ffn_gain[None, :]
    m_out, m_down = magnitude_out[None, :], magnitude_down[None, :]
    at_qkv, at_gu = adapt_a_qkv.transpose(0, 2, 1), adapt_a_gu.transpose(0, 2, 1)
    at_out, at_down = adapt_a_out.T, adapt_a_down.T

    q, k, v, h1, pre, low, norm_qkv, v_qkv, norms, v_out, v_down, norm_gu, v_gu = front(
        sizes, x, gain1, cos, sin, (base_qkv, at_qkv, adapt_b_qkv, magnitude_qkv), (base_out, at_out, adapt_b_out),
        (base_down, at_down, adapt_b_down), (base_gu, at_gu, adapt_b_gu),
    )
    q, k, v = q.reshape(-1, HD), k.reshape(length, HD), v.reshape(length, HD)
    o, lse = attend(q, k, v, low_block, block_at, start, place, group)
    out_pre, attn, low_out = out_project(sizes, o.reshape(-1, group, HD), base_out, at_out, adapt_b_out)
    dh2, down_part, s_down, ga_gu, gb_gu, gm_gu, g_gain2, ga_down, gb_down = ffn(
        out_pre, x, m_out, norms, gain2, (base_gu, at_gu, adapt_b_gu), magnitude_gu, norm_gu, v_gu,
        (base_down, at_down, adapt_b_down), m_down, dy,
    )
    dh2, s_down = middle(sizes, dh2, s_down)
    down_part, dh2 = lax.optimization_barrier((down_part, dh2))
    down_pre = lax.psum(down_part, "heads")
    do, dx2, ga_out, gb_out, gm_out = out_back(
        sizes, dh2, x, out_pre, dy, gain2, m_out, norms, base_out, at_out, adapt_b_out, v_out, attn, low_out
    )
    dq, dk, dv = attend_back(
        q, k, v, o, do.reshape(-1, HD), lse, low_block, block_at, start, place, group
    )
    dh1, wide, narrow, hid = last(
        sizes,
        (
            dq.reshape(-1, group, HD), dk.reshape(-1, group, HD), dv.reshape(-1, group, HD), cos, sin, h1, pre,
            low, gain1, at_qkv, adapt_b_qkv, magnitude_qkv, norm_qkv, v_qkv, ga_gu, gb_out, gb_down, g_gain2,
            gm_out, s_down, ga_out, gb_gu, gm_gu, ga_down, m_down, norms, at_down, adapt_b_down, v_down,
        ),
        base_qkv,
        base_down,
    )
    xf = x.astype(F32)
    inverse_one = lax.rsqrt(jnp.mean(xf * xf, axis=-1, keepdims=True) + NORM_EPS)
    scaled = dh1.astype(F32) * gain1
    dx = dx2.astype(F32) + inverse_one * scaled
    dx = dx - xf * inverse_one**3 * jnp.mean(scaled * xf, axis=-1, keepdims=True)
    x2 = xf + out_pre.astype(F32) * (m_out / norms[0:1])
    mixed = (x2 + down_pre.astype(F32) * (m_down / norms[1:2])).astype(BF16)
    wide, narrow, hid = wide.astype(F32), narrow.astype(F32), hid.astype(F32)
    return (
        mixed.reshape(rows_n, group, width),
        dx.reshape(rows_n, group, width),
        wide[112],
        wide[:48].reshape(3, RANK, width).transpose(0, 2, 1),
        narrow[:48].reshape(3, RANK, local),
        narrow[48:51],
        narrow[64:80].T,
        wide[80:96],
        wide[114],
        wide[113],
        wide[48:80].reshape(2, RANK, width).transpose(0, 2, 1),
        hid[:32].reshape(2, RANK, -1),
        hid[32:34],
        hid[48:64].T,
        wide[96:112],
        wide[115],
    )


def solution(mesh):
    in_specs = (
        P(None, "seq", None), P(), P(None, None, "heads"), P(), P(None, None, "heads"), P(None, "heads"),
        P("heads", None), P("heads", None), P(), P(), P(), P(None, None, "heads"), P(),
        P(None, None, "heads"), P(None, "heads"), P("heads", None), P("heads", None), P(), P(), P(),
        P(None, "seq", None),
    )
    out_specs = (
        P(None, "seq", None), P(None, "seq", None), P(), P(), P(None, None, "heads"), P(None, "heads"),
        P("heads", None), P(), P(), P(), P(), P(None, None, "heads"), P(None, "heads"),
        P("heads", None), P(), P(),
    )
    return jax.shard_map(
        per_device, mesh=mesh, in_specs=in_specs, out_specs=out_specs, check_vma=False
    )
```

time: 849 us -> 439 us (0.52)
  waiting for transfers between devices: 172 us -> 0.02 us
  matrix products: 139 us -> 0 us
  other arithmetic: 83.7 us -> 14.2 us
  blocking collectives: 20.8 us -> 0 us
    psum x4 -> x1, waiting for transfers between devices: 171 us -> 0.01 us  [per_device(): down_pre = lax.psum(down_part, 'heads')]
    dot_general x84 -> x0, matrix products: 139 us -> none  [dot(): lax.dot_general(a.astype(BF16), b.astype(BF16), dims, preferred_element_t...]
    reduce_sum x12 -> x2, other arithmetic: 29.1 us -> 2.89 us  [the longest x1 2.41 us: per_device(): jnp.mean(scaled * xf, axis=-1, keepdims=True)]
    convert_element_type x23 -> x2, other arithmetic: 23.4 us -> 0.04 us  [per_device(): wide, narrow, hid = (wide.astype(F32), narrow.astype(F32), hid.astype(F32))]
    psum x1 -> x0, blocking collectives: 20.8 us -> none  [per_device(): out_squares, down_squares = lax.psum((out_squares, down_squares), 'heads')]
    unnamed x289 -> x92, local copies, waits for them, and re-layouts: 11.6 us -> 20.2 us
    transpose x7 -> x0, other arithmetic: 8.56 us -> none  [the longest x2 2.4 us: per_device(): both[0].transpose(0, 2, 1)]
    pallas_call x9 -> x8, Pallas kernels: 385 us -> 383 us  [the longest x1 109 us: last(): pl.pallas_call(functools.partial(last_kernel, *sizes), out_shape=[shape(c...]
  transfers between devices with their start and end apart: 4 -> 1, of which waited for: 2 -> 0; matrix products, arithmetic and copies ran while one was open for 8% -> 2% of each run, Pallas kernels for 15% -> 32%
where the time goes in v2:
time: 439 us
  Pallas kernels  383 us (87%)
  local copies, waits for them, and re-layouts  27 us (6%)
  between operations  14.6 us (3%)
  other arithmetic  14.2 us (3%)
    pallas_call x1, Pallas kernels, last(): pl.pallas_call(functools.partial(last_kernel, *sizes), out_shape=[shape(c...  109 us
    pallas_call x1, Pallas kernels, out_project(): pl.pallas_call(functools.partial(out_kernel, *sizes), out_shape=[shape(co...  74.7 us
    pallas_call x1, Pallas kernels, middle(): pl.pallas_call(functools.partial(middle_kernel, depth), out_shape=[shape(...  66 us
    pallas_call x1, Pallas kernels, ffn(): pl.pallas_call(ffn_kernel, out_shape=[shape(count, width), shape(count, w...  45.6 us
    pallas_call x1, Pallas kernels, front(): pl.pallas_call(functools.partial(front_kernel, *sizes), out_shape=[shape(...  39.2 us
    unnamed x92, local copies, waits for them, and re-layouts  20.2 us
    pallas_call x1, Pallas kernels, out_back(): pl.pallas_call(functools.partial(out_back_kernel, *sizes), out_shape=[sha...  16.8 us
    pallas_call x1, Pallas kernels, attend_back(): pl.pallas_call(functools.partial(attend_back_kernel, block), out_shape=[s...  16.5 us
  transfers between devices with their start and end apart: 1, of which 0 were waited for; matrix products, arithmetic and copies ran while one was open for 2% of the time, Pallas kernels for 32%

profile of v2, /device:TPU:0, one launch (start us, length us, event | category | flops | bytes accessed | tf_op | source)
XLA Modules:
  0.0 438.6 jit_solution(3835515603614304883)
XLA Ops:
  7.2 0.0 all-reduce.2.cloned.1.call-start
  7.3 0.8 select_reduce_fusion.2
  8.1 0.8 select_reduce_fusion.4
  8.8 0.1 select_reduce_fusion.1
  9.0 0.1 fusion.6
  9.0 0.1 select_reduce_fusion
  9.1 0.0 copy-start.24
  9.2 0.1 slice_reduce_fusion
  9.3 0.0 copy-start.26
  9.3 1.0 fusion.5
  10.3 1.0 pad_maximum_fusion
  11.3 39.2 %shard_map.324 = (bf16[8,256,128]{2,1,0:T(8,128)(2,1)}, bf16[8,256,128]{2,1,0:T(8,128)(2,1)}, bf16[8,256,128]{2,1,0:T(8,128)(2,1)}, bf16[560,2048]{1,0:T(8,128)(...) custom-call(bf16[512,2048]{1,0:T(8,128)(2,1)} %bitcast.55, ...), custom_call_target="tpu_custom_call" | custom-call | tf_op jit(solution)/shard_map/pallas_call | solution.py:400
  50.5 1.0 copy-done.7
  51.6 1.0 copy-done.9
  52.6 1.0 copy-done.11
  53.7 14.9 %shard_map.325 = (bf16[2048,128]{1,0:T(8,128)(2,1)S(1)}, f32[1,2048]{1,0:T(1,128)S(1)}) custom-call(s32[8]{0:T(128)S(1)} %and_select_fusion.low_ref, s32[8]{0:T(128)S(1)} %iota.53.high_ref, bf16[2048,128]{1,0:T(8,128)(2,1)S(1)} %bitcast.60, bf16[2048,128]{1,0:T(8,128)(2,1)S(1)} %bitcast.62, bf16[2048,128]{1,0:T(8,128)(2,1)S(1)} %bitcast.64, ...), custom_call_target="tpu_custom_call" | custom-call | tf_op jit(solution)/shard_map/pallas_call | solution.py:460
  68.5 0.0 copy-start.34
  68.5 0.6 copy-done.34
  69.1 74.7 %shard_map.326 = (bf16[512,2048]{1,0:T(8,128)(2,1)S(1)}, bf16[512,512]{1,0:T(8,128)(2,1)S(1)}, bf16[512,16]{1,0:T(8,128)(2,1)S(1)}) custom-call(bf16[8,256,128]{2,1,0:T(8,128)(2,1)S(1)} %bitcast.66, bf16[512,2048]{1,0:T(8,128)(2,1)S(1)} %copy-done.1, bf16[16,512]{1,0:T(8,128)(2,1)S(1)} %bitcast.72, bf16[16,2048]{1,0:T(8,128)(2,1)S(1)} %copy-done.17), custom_call_target="tpu_custom_call" | custom-call | tf_op jit(solution)/shard_map/pallas_call | solution.py:549
  143.9 0.0 copy-start.3
  143.9 1.3 copy-done.3
  145.2 45.6 %shard_map.327 = (bf16[512,2048]{1,0:T(8,128)(2,1)}, bf16[512,2048]{1,0:T(8,128)(2,1)}, f32[8,2048]{1,0:T(8,128)}, f32[2,16,2048]{2,1,0:T(8,128)}, f32[2,16,1408...) custom-call(bf16[512,2048]{1,0:T(8,128)(2,1)} %copy-done.3, ...), custom_call_target="tpu_custom_call" | custom-call | tf_op jit(solution)/shard_map/pallas_call | solution.py:667
  190.9 0.0 copy-start
  190.9 0.0 copy-start.6
  190.9 1.7 copy-done.6
  192.6 0.8 copy-done.31
  193.4 66.0 %shard_map.328 = (bf16[512,2048]{1,0:T(8,128)(2,1)S(1)}, f32[8,2048]{1,0:T(8,128)S(1)}) custom-call(bf16[512,2048]{1,0:T(8,128)(2,1)S(1)} %copy-done.6, f32[8,2048]{1,0:T(8,128)S(1)} %copy-done.31), custom_call_target="tpu_custom_call" | custom-call | tf_op jit(solution)/shard_map/pallas_call | solution.py:703
  259.5 0.0 copy-start.13
  259.5 1.3 copy-done.13
  260.8 0.6 copy-done.30
  261.4 0.0 all-reduce.2.cloned.1.call-update
  261.5 0.5 multiply_reduce_fusion
  262.0 1.6 copy-done.2
  263.6 1.6 copy-done.4
  265.2 1.9 copy-done.5
  267.1 1.6 copy-done.14
  268.7 0.7 copy-done.28
  269.4 0.7 copy-done.33
  270.1 0.0 copy-start.27
  270.1 0.0 copy-start.35
  270.1 16.8 %shard_map.329 = (bf16[8,256,128]{2,1,0:T(8,128)(2,1)S(1)}, bf16[512,2048]{1,0:T(8,128)(2,1)S(1)}, f32[16,512]{1,0:T(8,128)S(1)}, f32[16,2048]{1,0:T(8,128)S(1)}, f32[1,2048]{1,0:T(1,128)S(1)}) custom-call(bf16[512,2048]{1,0:T(8,128)(2,1)S(1)} %copy-done.14, bf16[512,2048]{1,0:T(8,128)(2,1)S(1)} %bitcast.57, bf16[512,2048]{1,0:T(8,128)(2,1)S(1)} %copy-done.4, ...), custom_call_target="tpu_custom_call" | custom-call | tf_op jit(solution)/shard_map/pallas_call | solution.py:768
  286.9 0.0 copy-start.23
  286.9 0.0 copy-start.32
  287.0 16.5 %shard_map.330 = (bf16[2048,128]{1,0:T(8,128)(2,1)S(1)}, bf16[2048,128]{1,0:T(8,128)(2,1)S(1)}, bf16[2048,128]{1,0:T(8,128)(2,1)S(1)}) custom-call(s32[8]{0:T(128)S(1)} %copy-done.38, s32[8]{0:T(128)S(1)} %iota.56.high_ref, bf16[2048,128]{1,0:T(8,128)(2,1)S(1)} %bitcast.61, bf16[2048,128]{1,0:T(8,128)(2,1)S(1)} %bitcast.63, bf16[2048,128]{1,0:T(8,128)(2,1)S(1)} %bitcast.65, ...), custom_call_target="tpu_custom_call" | custom-call | tf_op jit(solution)/shard_map/pallas_call | solution.py:507
  303.5 0.0 copy-start.18
  303.5 0.8 copy-done.18
  304.3 0.8 copy-done.19
  305.2 0.8 copy-done.20
  306.0 109.1 %shard_map.331 = (bf16[512,2048]{1,0:T(8,128)(2,1)}, bf16[128,2048]{1,0:T(8,128)(2,1)}, bf16[80,512]{1,0:T(8,128)(2,1)}, bf16[64,1408]{1,0:T(8,128)(2,1)}) custom-call(bf16[8,256,128]{2,1,0:T(8,128)(2,1)} %bitcast.67, bf16[8,256,128]{2,1,0:T(8,128)(2,1)} %bitcast.68, bf16[8,256,128]{2,1,0:T(8,128)(2,1)} %bitcast.69, f32[512,128]{1,0:T(8,128)} %get-tuple-element.120.cos, ...), custom_call_target="tpu_custom_call" | custom-call | tf_op jit(solution)/shard_map/pallas_call | solution.py:992
  415.1 0.0 copy-start.29
  415.1 0.0 copy-start.43
  415.1 2.4 fusion.4
  417.6 0.8 slice.70
  418.4 0.7 slice.77
  419.1 0.7 slice.78
  419.8 0.6 slice.71
  420.5 0.6 slice.79
  421.1 0.6 slice.72
  421.7 0.6 slice_bitcast_fusion.1
  422.3 0.6 fusion.8
  422.9 0.9 slice_divide_fusion.1
  423.9 0.6 slice_bitcast_fusion
  424.5 0.7 fusion.9
  425.2 6.5 %fusion.3 = (f32[512,2048]{1,0:T(8,128)}, bf16[512,2048]{1,0:T(8,128)(2,1)}) fusion(bf16[512,2048]{1,0:T(8,128)(2,1)} %get-tuple-element.98, bf16[512,2048]{1,0:T(8,128)(2,1)} %copy-done.15, f32[512]{0:T(512)S(1)} %broadcast_multiply_fusion, f32[512]{0:T(512)S(1)} %multiply_multiply_fusion, f32[2048]{0:T(1024)S(1)} %copy-done.42, f32[512]{0:T(512)S(1)} %bitcast.105, ...), kind=kLoop, calls=%fused_computation.6 | loop fusion | flops 16777216 | bytes 16807936 | tf_op jit(solution)/shard_map/sub | solution.py:1101
  (76 shorter events, 0.3 us)
Async XLA Ops:
  7.2 418.1 %all-reduce.2.cloned.1.call-start = ((), (), s32[]{:S(2)}) async-start(), calls=%async_computation | async-start | bytes 4194304 | tf_op jit(solution)/shard_map/psum | solution.py:1080
  9.1 41.4 %copy-start.24 = (s32[2048]{0:T(1024)}, s32[2048]{0:T(1024)S(1)}, u32[]{:S(2)}) copy-start(s32[2048]{0:T(1024)S(1)} %select_reduce_fusion) | copy-start | bytes 24580
  9.3 41.2 %copy-start.37 = (s32[8]{0:T(128)}, s32[8]{0:T(128)S(1)}, u32[]{:S(2)}) copy-start(s32[8]{0:T(128)S(1)} %and_select_fusion.low_ref) | copy-start | bytes 100
  9.3 41.2 %copy-start.26 = (s32[1,1,8,256]{3,1,2,0:T(1,128)}, s32[1,1,8,256]{3,1,2,0:T(1,128)S(1)}, u32[]{:S(2)}) copy-start(s32[1,1,8,256]{3,1,2,0:T(1,128)S(1)} %copy.39) | copy-start | bytes 24580
  11.3 57.8 %copy-start.1 = (bf16[512,2048]{1,0:T(8,128)(2,1)S(1)}, bf16[512,2048]{1,0:T(8,128)(2,1)}, u32[]{:S(2)}) copy-start(bf16[512,2048]{1,0:T(8,128)(2,1)} %w.3) | copy-start | bytes 6291460
  11.3 57.8 %copy-start.17 = (bf16[16,2048]{1,0:T(8,128)(2,1)S(1)}, bf16[16,2048]{1,0:T(8,128)(2,1)}, u32[]{:S(2)}) copy-start(bf16[16,2048]{1,0:T(8,128)(2,1)} %b.4) | copy-start | bytes 196612
  11.3 57.8 %copy-start.21 = (bf16[512,16]{0,1:T(8,128)(2,1)S(1)}, bf16[512,16]{0,1:T(8,128)(2,1)}, u32[]{:S(2)}) copy-start(bf16[512,16]{0,1:T(8,128)(2,1)} %param.28) | copy-start | bytes 49156
  50.5 1.0 copy-start.7
  51.6 1.0 copy-start.9
  52.6 1.0 copy-start.11
  68.5 0.6 copy-start.34
  143.9 1.3 copy-start.3
  145.2 116.7 %copy-start.16 = (f32[8,2048]{1,0:T(8,128)S(1)}, f32[8,2048]{1,0:T(8,128)}, u32[]{:S(2)}) copy-start(f32[8,2048]{1,0:T(8,128)} %get-tuple-element.64.norms) | copy-start | bytes 196612
  145.2 116.8 %copy-start.22 = (f32[16,2048]{1,0:T(8,128)S(1)}, f32[16,2048]{1,0:T(8,128)}, u32[]{:S(2)}) copy-start(f32[16,2048]{1,0:T(8,128)} %get-tuple-element.73.v_out) | copy-start | bytes 393220
  190.9 70.6 %copy-start = (bf16[2,256,2048]{2,1,0:T(8,128)(2,1)S(1)}, bf16[2,256,2048]{2,1,0:T(8,128)(2,1)}, u32[]{:S(2)}) copy-start(bf16[2,256,2048]{2,1,0:T(8,128)(2,1)} %param.21) | copy-start | bytes 6291460
  190.9 1.7 copy-start.6
  192.6 0.8 copy-start.31
  259.5 1.3 copy-start.13
  260.8 0.6 copy-start.30
  262.0 1.6 copy-start.2
  263.6 1.6 copy-start.4
  265.2 1.9 copy-start.5
  267.1 1.6 copy-start.14
  268.7 0.7 copy-start.28
  269.4 0.7 copy-start.33
  270.1 16.9 %copy-start.8 = (bf16[8,256,128]{2,1,0:T(8,128)(2,1)S(1)}, bf16[8,256,128]{2,1,0:T(8,128)(2,1)}, u32[]{:S(2)}) copy-start(bf16[8,256,128]{2,1,0:T(8,128)(2,1)} %get-tuple-element.59) | copy-start | bytes 1572868
  270.1 16.9 %copy-start.10 = (bf16[8,256,128]{2,1,0:T(8,128)(2,1)S(1)}, bf16[8,256,128]{2,1,0:T(8,128)(2,1)}, u32[]{:S(2)}) copy-start(bf16[8,256,128]{2,1,0:T(8,128)(2,1)} %get-tuple-element.60) | copy-start | bytes 1572868
  270.1 16.9 %copy-start.12 = (bf16[8,256,128]{2,1,0:T(8,128)(2,1)S(1)}, bf16[8,256,128]{2,1,0:T(8,128)(2,1)}, u32[]{:S(2)}) copy-start(bf16[8,256,128]{2,1,0:T(8,128)(2,1)} %get-tuple-element.61) | copy-start | bytes 1572868
  270.1 16.9 %copy-start.25 = (s32[2048]{0:T(1024)S(1)}, s32[2048]{0:T(1024)}, u32[]{:S(2)}) copy-start(s32[2048]{0:T(1024)} %copy-done.24) | copy-start | bytes 24580
  270.1 16.9 %copy-start.27 = (s32[1,1,8,256]{3,1,2,0:T(1,128)S(1)}, s32[1,1,8,256]{3,1,2,0:T(1,128)}, u32[]{:S(2)}) copy-start(s32[1,1,8,256]{3,1,2,0:T(1,128)} %copy-done.26) | copy-start | bytes 24580
  270.1 16.9 %copy-start.35 = (f32[1,2048]{1,0:T(1,128)S(1)}, f32[1,2048]{1,0:T(1,128)}, u32[]{:S(2)}) copy-start(f32[1,2048]{1,0:T(1,128)} %copy-done.34) | copy-start | bytes 24580
  270.1 16.9 %copy-start.38 = (s32[8]{0:T(128)S(1)}, s32[8]{0:T(128)}, u32[]{:S(2)}) copy-start(s32[8]{0:T(128)} %copy-done.37) | copy-start | bytes 100
  286.9 16.7 %copy-start.15 = (bf16[512,2048]{1,0:T(8,128)(2,1)}, bf16[512,2048]{1,0:T(8,128)(2,1)S(1)}, u32[]{:S(2)}) copy-start(bf16[512,2048]{1,0:T(8,128)(2,1)S(1)} %get-tuple-element.76) | copy-start | bytes 6291460
  286.9 19.1 %copy-start.23 = (f32[16,2048]{1,0:T(8,128)}, f32[16,2048]{1,0:T(8,128)S(1)}, u32[]{:S(2)}) copy-start(f32[16,2048]{1,0:T(8,128)S(1)} %get-tuple-element.88.gb_out) | copy-start | bytes 393220
  286.9 19.1 %copy-start.32 = (f32[16,512]{1,0:T(8,128)}, f32[16,512]{1,0:T(8,128)S(1)}, u32[]{:S(2)}) copy-start(f32[16,512]{1,0:T(8,128)S(1)} %get-tuple-element.93.ga_out) | copy-start | bytes 98308
  286.9 19.1 %copy-start.36 = (f32[1,2048]{1,0:T(1,128)}, f32[1,2048]{1,0:T(1,128)S(1)}, u32[]{:S(2)}) copy-start(f32[1,2048]{1,0:T(1,128)S(1)} %get-tuple-element.91.gm_out) | copy-start | bytes 24580
  303.5 0.8 copy-start.18
  304.3 0.8 copy-start.19
  305.2 0.8 copy-start.20
  306.0 109.1 %copy-start.42 = (f32[2048]{0:T(1024)S(1)}, f32[2048]{0:T(1024)}, u32[]{:S(2)}) copy-start(f32[2048]{0:T(1024)} %param.22) | copy-start | bytes 24580
  415.1 2.5 copy-start.39
  415.1 4.0 copy-start.40
  415.1 4.7 %copy-start.41 = (bf16[80,512]{1,0:T(8,128)(2,1)S(1)}, bf16[80,512]{1,0:T(8,128)(2,1)}, u32[]{:S(2)}) copy-start(bf16[80,512]{1,0:T(8,128)(2,1)} %get-tuple-element.100) | copy-start | bytes 245764
  415.1 7.8 %copy-start.29 = (f32[2048]{0:T(1024)S(1)}, f32[2048]{0:T(1024)}, u32[]{:S(2)}) copy-start(f32[2048]{0:T(1024)} %param.30) | copy-start | bytes 24580
  415.1 7.8 %copy-start.43 = (f32[2048]{0:T(1024)S(1)}, f32[2048]{0:T(1024)}, u32[]{:S(2)}) copy-start(f32[2048]{0:T(1024)} %param.39) | copy-start | bytes 24580
Sparse Core Ops, SparseCore 0:
  261.6 86.0 all-reduce.1
